TPU v7x, 32 devices: a whole 2x2x4 slice. The times are simulated.
32 devices in a mesh: row: 8 (over y, x, core), col: 4 (over z).
Axes of the slice: x: 2, y: 2, z: 4, core: 2. Of those that a mesh axis runs over, the one named last changes fastest.
Arguments:
- objects: float32 [2, 2, 1024, 1024], P(None, None, 'row', 'col'), as said below
- probe_modes: float32 [4, 2, 128, 128], replicated, may hold values from -3 to 3
- intensities: float32 [8, 4, 2, 128, 128], P('row', 'col'), may hold values from 0 to 2
- positions: int32 [8, 4, 2, 2], P('row', 'col'), may hold values from 0 to 896, as said below
- counts: int32 [8, 4], P('row', 'col'), may hold values from 0 to 2, as said below
Outputs:
- refined_object: float32 [2, 2, 1024, 1024], P(None, None, 'row', 'col')
- refined_probe: float32 [4, 2, 128, 128], replicated
Inputs may be any that keep to these rules, and one draw needn't show every extreme that they name: `positions`: for the pattern slot [i, j, k], the row of its top-left pixel plus 128 / 2 lies in [i * 128, (i + 1) * 128) and the column plus 128 / 2 in [j * 256, (j + 1) * 256); every patch lies inside the object; slot 0 of the first tile starts at pixel (0, 0) and slot 0 of the last tile ends at the object's last row and column. The live slots of a tile are its first counts[i, j] slots; some tile has all 2 live and some tile has none. `objects`: every entry lies in [-1.5, 1.5].
All inputs are finite; a program needn't handle non-finite values.
Results may differ from a plain program's by a relative error of at most 0.0003.
Values sent between devices are 32-bit elements; how exact they have to be, the bound alone decides.
A program may use at most 64 MiB of HBM per device.

v0:
```python
import math

import jax
import jax.numpy as jnp
from jax import lax
from jax.sharding import PartitionSpec as P

ITERS = 2


highest = lax.Precision.HIGHEST


def extended_2(value, sides, width):
    for axis, dim in sides:
        size, length = (lax.axis_size(axis), value.shape[dim])
        up = [(i, (i + 1) % size) for i in range(size - 1)]
        down = [(j, i) for i, j in up]
        last = lax.slice_in_dim(value, length - width, length, axis=dim)
        initial = lax.slice_in_dim(value, 0, width, axis=dim)
        before = lax.ppermute(last, axis, up)
        after = lax.ppermute(initial, axis, down)
        value = jnp.concatenate([before, value, after], axis=dim)
    return value


def block_table(upper_left, upper_right, lower_left, lower_right):
    return jnp.stack([jnp.stack([upper_left, upper_right]), jnp.stack([lower_left, lower_right])])


def fourier_tables(width):
    index = jnp.arange(width, dtype=jnp.int32)
    product = index[:, None] * index[None, :] % width
    angle = product.astype(jnp.float32) * (-2.0 * math.pi / width)
    scale = 1.0 / math.sqrt(width)
    middle = width // 2
    frequency = ((index + middle) % width - middle).astype(jnp.float32)
    phase = (frequency[:, None] ** 2 + frequency[None, :] ** 2) * (-4.0 * math.pi / (width * width))
    cosine = jnp.cos(angle) * scale
    sine = jnp.sin(angle) * scale
    forward_left = block_table(cosine, -sine, sine, cosine)
    forward_right = block_table(cosine, sine, -sine, cosine)
    inverse_left = block_table(cosine, sine, -sine, cosine)
    inverse_right = block_table(cosine, -sine, sine, cosine)
    return (
        forward_left,
        forward_right,
        inverse_left,
        inverse_right,
        jnp.cos(phase),
        jnp.sin(phase),
    )


def fourier_field(field, tables, direction):
    if direction > 0:
        left_table, right_table = (tables[0], tables[1])
    else:
        left_table, right_table = (tables[2], tables[3])
    upper = jnp.einsum("pqab,kmqbc->kmpac", left_table, field, precision=highest)
    return jnp.einsum("kmqab,qpbc->kmpac", upper, right_table, precision=highest)


def complex_product(first, second):
    real_part = first[:, :, 0] * second[:, :, 0] - first[:, :, 1] * second[:, :, 1]
    imag_part = first[:, :, 0] * second[:, :, 1] + first[:, :, 1] * second[:, :, 0]
    return jnp.stack([real_part, imag_part], axis=2)


def conj_product(first, second):
    real_part = first[:, :, 0] * second[:, :, 0] + first[:, :, 1] * second[:, :, 1]
    imag_part = first[:, :, 0] * second[:, :, 1] - first[:, :, 1] * second[:, :, 0]
    return jnp.stack([real_part, imag_part], axis=2)


def propagate(field, tables, direction):
    spectrum = fourier_field(field, tables, 1.0)
    kernel = jnp.stack([tables[4], tables[5] * direction])[None, None]
    return fourier_field(complex_product(spectrum, kernel), tables, -1.0)


def pattern_terms(probe_modes, patches, measured, live_mask, tables):
    slot_count = patches.shape[0]
    layers = patches.shape[1]
    wave = jnp.broadcast_to(probe_modes[None], (slot_count,) + probe_modes.shape)
    inputs = []
    for layer_index in range(layers):
        obj = patches[:, layer_index][:, None]
        inputs.append(wave)
        exit_wave = complex_product(wave, obj)
        if layer_index < layers - 1:
            wave = propagate(exit_wave, tables, 1.0)
        else:
            far = fourier_field(exit_wave, tables, 1.0)
    intensity = jnp.sum(far * far, axis=(1, 2))
    weight = (2.0 * (intensity - measured))[:, None, None]
    grad = fourier_field(weight * far, tables, -1.0)
    slice_grads = [None] * layers
    for layer_index in reversed(range(layers)):
        obj = patches[:, layer_index][:, None]
        slice_grads[layer_index] = jnp.sum(conj_product(inputs[layer_index], grad), axis=1)
        back = conj_product(obj, grad)
        if layer_index > 0:
            grad = propagate(back, tables, -1.0)
    weights = live_mask[:, None, None, None, None]
    object_grads = jnp.stack(slice_grads, axis=1) * weights
    probe_terms = jnp.sum(back * weights, axis=0)
    first = patches[:, 0]
    illumination = jnp.sum(jnp.sum(first * first, axis=1) * live_mask[:, None, None], axis=0)
    return (object_grads, probe_terms, illumination)


def fold_rims(padded, margin, offset, inner_rows, inner_cols):
    middle = padded[:, :, offset : offset + inner_rows, :]
    middle = middle.at[:, :, :margin, :].add(padded[:, :, :margin, :])
    middle = middle.at[:, :, inner_rows - margin :, :].add(
        padded[:, :, padded.shape[2] - margin :, :]
    )
    center = middle[:, :, :, offset : offset + inner_cols]
    center = center.at[:, :, :, :margin].add(middle[:, :, :, :margin])
    center = center.at[:, :, :, inner_cols - margin :].add(
        middle[:, :, :, middle.shape[3] - margin :]
    )
    return center


def fetch_bands(objects, margin):
    return extended_2(objects, (("row", 2), ("col", 3)), margin)


def return_rims(buffer, margin, tile_rows, tile_cols):
    padded = extended_2(buffer, (("row", 2), ("col", 3)), margin)
    return fold_rims(padded, margin, 2 * margin, tile_rows, tile_cols)


def local_pass(extended, probe_modes, measured, corners, live_mask, tables):
    layers = extended.shape[0]
    width = probe_modes.shape[-1]
    slot_count = corners.shape[0]

    def cut_patch(corner):
        start = (jnp.int32(0), jnp.int32(0), corner[0], corner[1])
        return lax.dynamic_slice(extended, start, (layers, 2, width, width))

    patches = jax.vmap(cut_patch)(corners)
    object_grads, probe_terms, illumination = pattern_terms(
        probe_modes, patches, measured, live_mask, tables
    )

    def place(slot_index, buffer):
        corner = corners[slot_index]
        start = (jnp.int32(0), jnp.int32(0), corner[0], corner[1])
        present = lax.dynamic_slice(buffer, start, (layers, 2, width, width))
        return lax.dynamic_update_slice(buffer, present + object_grads[slot_index], start)

    buffer = lax.fori_loop(0, slot_count, place, jnp.zeros(extended.shape, jnp.float32))
    probe_total, light_total = lax.psum((probe_terms, illumination), ("row", "col"))
    new_modes = probe_modes - 0.25 * probe_total / jnp.sqrt(light_total)
    return (buffer, new_modes)


def body(objects, probe_modes, intensities, positions, counts):
    width = probe_modes.shape[-1]
    margin = width // 2
    tile_rows = objects.shape[2]
    tile_cols = objects.shape[3]
    slot_count = intensities.shape[2]
    tables = fourier_tables(width)
    anchor = jnp.stack([lax.axis_index("row") * tile_rows, lax.axis_index("col") * tile_cols])
    corners = positions[0, 0] - anchor[None, :] + margin
    live_mask = (jnp.arange(slot_count, dtype=jnp.int32) < counts[0, 0]).astype(jnp.float32)
    measured = intensities[0, 0]
    extended = fetch_bands(objects, margin)
    for step_index in range(ITERS):
        buffer, probe_modes = local_pass(
            extended, probe_modes, measured, corners, live_mask, tables
        )
        if step_index < ITERS - 1:
            padded = extended_2(buffer, (("row", 2), ("col", 3)), width)
            extended = extended - 0.1 * fold_rims(
                padded, width, width, tile_rows + width, tile_cols + width
            )
        else:
            interior = extended[:, :, margin : margin + tile_rows, margin : margin + tile_cols]
            objects = interior - 0.1 * return_rims(buffer, margin, tile_rows, tile_cols)
    return (objects, probe_modes)


def solution(mesh):
    return jax.shard_map(
        body,
        mesh=mesh,
        in_specs=(
            P(None, None, "row", "col"),
            P(),
            P("row", "col", None, None, None),
            P("row", "col", None, None),
            P("row", "col"),
        ),
        out_specs=(P(None, None, "row", "col"), P()),
        check_vma=False,
    )
```

profile of v0, /device:TPU:0, one launch (start us, length us, event | category | flops | bytes accessed | tf_op | source)
XLA Modules:
  0.0 483.3 jit_solution(8774689927589350137)
XLA Ops:
  9.6 2.5 collective-permute-start
  12.1 1.3 collective-permute-start.1
  19.3 3.5 collective-permute-start.2
  22.7 1.3 collective-permute-start.3
  25.3 1.8 copy.147
  27.1 1.6 slice_bitcast_fusion.13
  28.7 2.7 collective-permute-done.3
  31.3 2.6 pad_maximum_fusion.2
  34.0 7.1 %while.38 = (s32[]{:T(128)}, f32[2,2,256,384]{2,3,1,0:T(8,128)}, s32[2,4]{1,0:T(2,128)S(1)}, f32[2,2,2,128,128]{4,3,2,1,0:T(8,128)S(1)}, s32[]{:T(128)}) while((s32[]{:T(128)}, f32[2,2,256,384]{2,3,1,0:T(8,128)}, s32[2,4]{1,0:T(2,128)S(1)}, f32[2,2,2,128,128]{4,3,2,1,0:T(8,128)S(1)}, s32[]{:T(128)}) %tuple.190), condition=%wide.while_cond.8, body=%wide.while_body.8.sunk | while | flops 2 | bytes 1572989 | solution.py:143
  34.6 2.5 constant_dynamic-slice_fusion.24
  37.9 2.5 constant_dynamic-slice_fusion.24
  57.8 18.9 %while.36 = (s32[]{:T(128)}, f32[2,2,256,384]{2,3,1,0:T(8,128)S(1)}, s32[2,2]{1,0:T(2,128)S(1)}, f32[2,2,2,128,128]{3,4,0,2,1:T(8,128)}, s32[]{:T(128)}, /*index=5*/s32[]{:T(128)}, s32[]{:T(128)}, s32[]{:T(128)}) while((s32[]{:T(128)}, f32[2,2,256,384]{2,3,1,0:T(8,128)S(1)}, s32[2,2]{1,0:T(2,128)S(1)}, f32[2,2,2,128,128]{3,4,0,2,1:T(8,128)}, ...), condition=%wide.region_4.5_spmd, body=%wide.region_3.4_spmd.sunk | while | flops 65544 | bytes 3932365 | solution.py:156
  63.9 3.4 dynamic_update_slice.16
  73.3 3.4 dynamic_update_slice.16
  76.9 10.8 %collective-permute-start.4 = (f32[2,2,128,384]{2,3,1,0:T(8,128)S(1)}, f32[2,2,128,384]{2,3,1,0:T(8,128)S(1)}, u32[]{:S(2)}, u32[]{:S(2)}) collective-permute-start(f32[2,2,128,384]{2,3,1,0:T(8,128)S(1)} %get-tuple-element.387), channel_id=1, source_target_pairs={{0,4},{4,8},{8,12},{12,16},{16,20},{20,24},{24,28},{1,5},{5,9},{9,... | collective-permute-start | bytes 2359304 | tf_op jit(solution)/shard_map/ppermute | solution.py:21
  87.6 1.3 collective-permute-start.5
  89.8 5.1 %collective-permute-done.5 = f32[2,2,128,384]{2,3,1,0:T(8,128)S(1)} collective-permute-done((f32[2,2,128,384]{2,3,1,0:T(8,128)S(1)}, f32[2,2,128,384]{2,3,1,0:T(8,128)S(1)}, u32[]{:S(2)}, u32[]{:S(2)}) %collective-permute-start.5) | collective-permute-done | bytes 786464 | tf_op jit(solution)/shard_map/ppermute | solution.py:22
  95.1 1.6 copy-done.1
  96.7 1.6 fusion.60
  98.3 4.5 collective-permute-start.6
  102.8 1.3 collective-permute-start.7
  105.8 8.7 %collective-permute-done.6 = f32[2,2,512,128]{2,3,1,0:T(8,128)} collective-permute-done((f32[2,2,512,128]{2,3,1,0:T(8,128)}, f32[2,2,512,128]{2,3,1,0:T(8,128)}, u32[]{:S(2)}, u32[]{:S(2)}) %collective-permute-start.6) | collective-permute-done | bytes 1048608 | tf_op jit(solution)/shard_map/ppermute | solution.py:21
  114.4 5.4 %collective-permute-done.7 = f32[2,2,512,128]{2,3,1,0:T(8,128)} collective-permute-done((f32[2,2,512,128]{2,3,1,0:T(8,128)}, f32[2,2,512,128]{2,3,1,0:T(8,128)}, u32[]{:S(2)}, u32[]{:S(2)}) %collective-permute-start.7) | collective-permute-done | bytes 1048608 | tf_op jit(solution)/shard_map/ppermute | solution.py:22
  119.8 3.1 pad_maximum_fusion
  125.1 1.4 multiply_subtract_fusion
  126.6 4.4 while.39
  127.3 1.4 constant_dynamic-slice_fusion.26
  129.5 1.4 constant_dynamic-slice_fusion.26
  136.4 141.0 %all-reduce.7.cloned.1.call-done = (f32[4,2,128,128]{2,3,0,1:T(8,128)}, f32[128,128]{1,0:T(8,128)}) async-done(((f32[4,2,128,128]{2,3,0,1:T(8,128)}, f32[128,128]{1,0:T(8,128)}), (f32[4,2,128,128]{2,3,0,1:T(8,128)}, f32[128,128]{1,0:T(8,128)})) %all-reduce.7.cloned.1.call-update) | async-done | bytes 589840 | tf_op jit(solution)/shard_map/psum | solution.py:157
  291.7 1.3 convolution_bitcast_fusion.2
  295.5 15.2 %while.37 = (s32[]{:T(128)}, f32[2,2,256,384]{3,2,1,0:T(8,128)S(1)}, s32[2,2]{1,0:T(2,128)S(1)}, f32[2,2,2,128,128]{3,4,0,2,1:T(8,128)S(1)}, s32[]{:T(128)}, /*index=5*/s32[]{:T(128)}, s32[]{:T(128)}, s32[]{:T(128)}) while((s32[]{:T(128)}, f32[2,2,256,384]{3,2,1,0:T(8,128)S(1)}, s32[2,2]{1,0:T(2,128)S(1)}, ...), condition=%wide.region_14.15_spmd, body=%wide.region_13.14_spmd.sunk | while | flops 65544 | bytes 2359501 | solution.py:156
  299.9 3.2 dynamic_update_slice.17
  307.6 3.1 dynamic_update_slice.17
  311.5 3.3 collective-permute-start.8
  314.8 1.3 collective-permute-start.9
  317.1 1.6 copy.192
  318.7 1.4 copy.191
  320.1 1.5 copy.193
  321.7 1.2 pad_maximum_fusion.5
  322.9 3.4 collective-permute-start.10
  326.3 1.3 collective-permute-start.11
  327.6 120.7 %all-reduce.5.cloned.1.call-done = (f32[4,2,128,128]{2,3,0,1:T(8,128)}, f32[128,128]{1,0:T(8,128)}) async-done(((f32[4,2,128,128]{2,3,0,1:T(8,128)}, f32[128,128]{1,0:T(8,128)}), (f32[4,2,128,128]{2,3,0,1:T(8,128)}, f32[128,128]{1,0:T(8,128)})) %all-reduce.5.cloned.1.call-update) | async-done | bytes 589840 | tf_op jit(solution)/shard_map/psum | solution.py:157
  449.2 1.3 divide_subtract_fusion
  451.5 2.9 pad_maximum_fusion.1
  456.5 5.3 %scatter-add.34 = f32[2,2,128,512]{2,3,1,0:T(8,128)} dynamic-update-slice(f32[2,2,128,512]{2,3,1,0:T(8,128)} %slice.741, f32[2,2,64,512]{2,3,1,0:T(8,128)} %slice_add_fusion.3, s32[]{:T(128)} %constant.320.clone.1, s32[]{:T(128)} %constant.320.clone.1, s32[]{:T(128)} %constant.320.clone.1, s32[]{:T(128)} %constant.320.clone.1) | dynamic-update-slice | bytes 1048580 | tf_op jit(solution)/shard_map/scatter-add | solution.py:115
  461.8 2.8 slice_add_fusion.2
  464.6 6.1 %scatter-add.35 = f32[2,2,128,512]{2,3,1,0:T(8,128)} dynamic-update-slice(f32[2,2,128,512]{2,3,1,0:T(8,128)} %scatter-add.34, f32[2,2,64,512]{2,3,1,0:T(8,128)} %slice_add_fusion.2, s32[]{:T(128)} %constant.320.clone.1, s32[]{:T(128)} %constant.320.clone.1, s32[]{:T(128)} %constant.327.clone.1, s32[]{:T(128)} %constant.320.clone.1) | dynamic-update-slice | bytes 1048580 | tf_op jit(solution)/shard_map/scatter-add | solution.py:116
  473.8 1.4 slice_subtract_fusion
  (239 shorter events, 71.1 us)
Async XLA Ops:
  7.2 7.1 %copy-start.36 = (s32[1,1,2,2]{3,2,1,0:T(2,128)S(1)}, s32[1,1,2,2]{3,2,1,0:T(2,128)}, u32[]{:S(2)}) copy-start(s32[1,1,2,2]{3,2,1,0:T(2,128)} %param.28) | copy-start | bytes 52
  7.2 270.2 %all-reduce.7.cloned.1.call-start = ((), (), s32[]{:S(2)}) async-start(), calls=%async_computation.1 | async-start | bytes 1179648 | tf_op jit(solution)/shard_map/psum | solution.py:157
  9.6 6.7 %copy-start.21 = (f32[4,2,128,128]{3,2,1,0:T(8,128)S(1)}, f32[4,2,128,128]{3,2,1,0:T(8,128)}, u32[]{:S(2)}) copy-start(f32[4,2,128,128]{3,2,1,0:T(8,128)} %param.26) | copy-start | bytes 1572868
  9.6 7.5 %collective-permute-start = (f32[2,2,64,256]{2,3,1,0:T(8,128)}, f32[2,2,64,256]{2,3,1,0:T(8,128)S(1)}, u32[]{:S(2)}, u32[]{:S(2)}) collective-permute-start(f32[2,2,64,256]{2,3,1,0:T(8,128)} %get-tuple-element.436), channel_id=1, source_target_pairs={{0,4},{4,8},{8,12},{12,16},{16,20},{20,24},{24,28},{1,5},{5,9},{9,... | collective-permute-start | bytes 786440 | tf_op jit(solution)/shard_map/ppermute | solution.py:21
  12.1 6.1 %collective-permute-start.1 = (f32[2,2,64,256]{2,3,1,0:T(8,128)}, f32[2,2,64,256]{2,3,1,0:T(8,128)S(1)}, u32[]{:S(2)}, u32[]{:S(2)}) collective-permute-start(f32[2,2,64,256]{2,3,1,0:T(8,128)} %get-tuple-element.437), channel_id=1, source_target_pairs={{4,0},{8,4},{12,8},{16,12},{20,16},{24,20},{28,24},{5,1},{9,5},{13... | collective-permute-start | bytes 786440 | tf_op jit(solution)/shard_map/ppermute | solution.py:22
  14.8 38.3 %copy-start.2 = (f32[1,2,128,128]{3,2,1,0:T(8,128)}, f32[1,2,128,128]{3,2,1,0:T(8,128)S(1)}, u32[]{:S(2)}) copy-start(f32[1,2,128,128]{3,2,1,0:T(8,128)S(1)} %get-tuple-element.449) | copy-start | bytes 393220
  14.9 34.7 %copy-start.7 = (f32[2,2,128,128,1,1]{3,2,1,0,5,4:T(8,128)}, f32[2,2,128,128,1,1]{3,2,1,0,5,4:T(8,128)S(1)}, u32[]{:S(2)}) copy-start(f32[2,2,128,128,1,1]{3,2,1,0,5,4:T(8,128)S(1)} %get-tuple-element.459) | copy-start | bytes 786436
  17.1 7.0 %copy-start.26 = (f32[4,128,128]{2,1,0:T(8,128)S(1)}, f32[4,128,128]{2,1,0:T(8,128)}, u32[]{:S(2)}) copy-start(f32[4,128,128]{2,1,0:T(8,128)} %get-tuple-element.434) | copy-start | bytes 786436
  17.1 14.2 %copy-start.10 = (f32[2,2,64,256]{2,3,1,0:T(8,128)}, f32[2,2,64,256]{2,3,1,0:T(8,128)S(1)}, u32[]{:S(2)}) copy-start(f32[2,2,64,256]{2,3,1,0:T(8,128)S(1)} %collective-permute-done) | copy-start | bytes 786436
  18.2 13.2 %copy-start.12 = (f32[2,2,64,256]{2,3,1,0:T(8,128)}, f32[2,2,64,256]{2,3,1,0:T(8,128)S(1)}, u32[]{:S(2)}) copy-start(f32[2,2,64,256]{2,3,1,0:T(8,128)S(1)} %collective-permute-done.1) | copy-start | bytes 786436
  19.3 9.4 %collective-permute-start.2 = (f32[2,2,256,64]{2,3,1,0:T(8,128)}, f32[2,2,256,64]{2,3,1,0:T(8,128)S(1)}, u32[]{:S(2)}, u32[]{:S(2)}) collective-permute-start(f32[2,2,256,64]{2,3,1,0:T(8,128)} %get-tuple-element.390), channel_id=1, source_target_pairs={{0,1},{1,2},{2,3},{4,5},{5,6},{6,7},{8,9},{9,10},{10,11},{12,13},{... | collective-permute-start | bytes 786440 | tf_op jit(solution)/shard_map/ppermute | solution.py:21
  22.7 8.6 %collective-permute-start.3 = (f32[2,2,256,64]{2,3,1,0:T(8,128)}, f32[2,2,256,64]{2,3,1,0:T(8,128)}, u32[]{:S(2)}, u32[]{:S(2)}) collective-permute-start(f32[2,2,256,64]{2,3,1,0:T(8,128)} %get-tuple-element.391), channel_id=1, source_target_pairs={{1,0},{2,1},{3,2},{5,4},{6,5},{7,6},{9,8},{10,9},{11,10},{13,12},{... | collective-permute-start | bytes 786440 | tf_op jit(solution)/shard_map/ppermute | solution.py:22
  25.3 16.3 %copy-start.16 = (f32[4,128,128]{1,2,0:T(8,128)}, f32[4,128,128]{1,2,0:T(8,128)S(1)}, u32[]{:S(2)}) copy-start(f32[4,128,128]{1,2,0:T(8,128)S(1)} %copy.136) | copy-start | bytes 786436
  28.6 5.3 %copy-start.24 = (f32[2,2,256,64]{2,3,1,0:T(8,128)}, f32[2,2,256,64]{2,3,1,0:T(8,128)S(1)}, u32[]{:S(2)}) copy-start(f32[2,2,256,64]{2,3,1,0:T(8,128)S(1)} %collective-permute-done.2) | copy-start | bytes 786436
  42.9 1.1 copy-start.31
  42.9 1.1 copy-start.33
  47.4 1.1 copy-start.22
  51.9 1.1 copy-start.27
  51.9 1.1 copy-start.29
  54.4 1.1 copy-start.17
  76.9 12.6 %collective-permute-start.4 = (f32[2,2,128,384]{2,3,1,0:T(8,128)S(1)}, f32[2,2,128,384]{2,3,1,0:T(8,128)S(1)}, u32[]{:S(2)}, u32[]{:S(2)}) collective-permute-start(f32[2,2,128,384]{2,3,1,0:T(8,128)S(1)} %get-tuple-element.387), channel_id=1, source_target_pairs={{0,4},{4,8},{8,12},{12,16},{16,20},{20,24},{24,28},{1,5},{5,9},{9,... | collective-permute-start | bytes 2359304 | tf_op jit(solution)/shard_map/ppermute | solution.py:21
  87.6 7.3 %collective-permute-start.5 = (f32[2,2,128,384]{2,3,1,0:T(8,128)S(1)}, f32[2,2,128,384]{2,3,1,0:T(8,128)S(1)}, u32[]{:S(2)}, u32[]{:S(2)}) collective-permute-start(f32[2,2,128,384]{2,3,1,0:T(8,128)S(1)} %get-tuple-element.386), channel_id=1, source_target_pairs={{4,0},{8,4},{12,8},{16,12},{20,16},{24,20},{28,24},{5,1},{9,5},{13... | collective-permute-start | bytes 2359304 | tf_op jit(solution)/shard_map/ppermute | solution.py:22
  95.1 1.6 copy-start.1
  96.7 7.4 %copy-start.18 = (f32[2,4,1,128,128]{3,4,2,1,0:T(8,128)S(1)}, f32[2,4,1,128,128]{3,4,2,1,0:T(8,128)}, u32[]{:S(2)}) copy-start(f32[2,4,1,128,128]{3,4,2,1,0:T(8,128)} %get-tuple-element.398) | copy-start | bytes 1572868
  96.7 7.4 %copy-start.19 = (f32[2,4,1,128,128]{3,4,2,1,0:T(8,128)S(1)}, f32[2,4,1,128,128]{3,4,2,1,0:T(8,128)}, u32[]{:S(2)}) copy-start(f32[2,4,1,128,128]{3,4,2,1,0:T(8,128)} %get-tuple-element.399) | copy-start | bytes 1572868
  98.3 6.8 %copy-start.15 = (f32[2,2,2,128,128]{4,3,2,1,0:T(8,128)S(1)}, f32[2,2,2,128,128]{4,3,2,1,0:T(8,128)}, u32[]{:S(2)}) copy-start(f32[2,2,2,128,128]{4,3,2,1,0:T(8,128)} %copy-done.14) | copy-start | bytes 1572868
  98.3 16.2 %collective-permute-start.6 = (f32[2,2,512,128]{2,3,1,0:T(8,128)}, f32[2,2,512,128]{2,3,1,0:T(8,128)}, u32[]{:S(2)}, u32[]{:S(2)}) collective-permute-start(f32[2,2,512,128]{2,3,1,0:T(8,128)} %get-tuple-element.376), channel_id=1, source_target_pairs={{0,1},{1,2},{2,3},{4,5},{5,6},{6,7},{8,9},{9,10},{10,11},{12,13},{... | collective-permute-start | bytes 3145736 | tf_op jit(solution)/shard_map/ppermute | solution.py:21
  102.8 17.0 %collective-permute-start.7 = (f32[2,2,512,128]{2,3,1,0:T(8,128)}, f32[2,2,512,128]{2,3,1,0:T(8,128)}, u32[]{:S(2)}, u32[]{:S(2)}) collective-permute-start(f32[2,2,512,128]{2,3,1,0:T(8,128)} %get-tuple-element.377), channel_id=1, source_target_pairs={{1,0},{2,1},{3,2},{5,4},{6,5},{7,6},{9,8},{10,9},{11,10},{13,12},{... | collective-permute-start | bytes 3145736 | tf_op jit(solution)/shard_map/ppermute | solution.py:22
  123.8 1.2 copy-start.13
  123.9 1.2 copy-start.25
  126.6 4.5 copy-start.35
  131.0 3.2 copy-start.4
  132.0 316.3 %all-reduce.5.cloned.1.call-start = ((), (), s32[]{:S(2)}) async-start(), calls=%async_computation | async-start | bytes 1179648 | tf_op jit(solution)/shard_map/psum | solution.py:157
  279.5 1.2 copy-start.9
  280.7 1.1 copy-start.32
  280.7 1.1 copy-start.34
  282.0 1.8 copy-start.8
  286.0 1.1 copy-start.23
  290.5 1.1 copy-start.28
  290.5 1.1 copy-start.30
  310.7 5.4 %copy-start.20 = (f32[2,4,1,128,128]{3,4,2,1,0:T(8,128)S(1)}, f32[2,4,1,128,128]{3,4,2,1,0:T(8,128)}, u32[]{:S(2)}) copy-start(f32[2,4,1,128,128]{3,4,2,1,0:T(8,128)} %get-tuple-element.393) | copy-start | bytes 1572868
  311.5 7.2 %collective-permute-start.8 = (f32[2,2,64,384]{3,2,1,0:T(8,128)}, f32[2,2,64,384]{3,2,1,0:T(8,128)}, u32[]{:S(2)}, u32[]{:S(2)}) collective-permute-start(f32[2,2,64,384]{3,2,1,0:T(8,128)} %get-tuple-element.382), channel_id=1, source_target_pairs={{0,4},{4,8},{8,12},{12,16},{16,20},{20,24},{24,28},{1,5},{5,9},{9,... | collective-permute-start | bytes 1179656 | tf_op jit(solution)/shard_map/ppermute | solution.py:21
  314.8 5.3 %collective-permute-start.9 = (f32[2,2,64,384]{3,2,1,0:T(8,128)S(1)}, f32[2,2,64,384]{3,2,1,0:T(8,128)}, u32[]{:S(2)}, u32[]{:S(2)}) collective-permute-start(f32[2,2,64,384]{3,2,1,0:T(8,128)S(1)} %get-tuple-element.383), channel_id=1, source_target_pairs={{4,0},{8,4},{12,8},{16,12},{20,16},{24,20},{28,24},{5,1},{9,5},{13... | collective-permute-start | bytes 1179656 | tf_op jit(solution)/shard_map/ppermute | solution.py:22
  318.7 3.0 copy-start
  320.1 131.4 %copy-start.5 = (f32[2,2,64,384]{2,3,1,0:T(8,128)}, f32[2,2,64,384]{2,3,1,0:T(8,128)S(1)}, u32[]{:S(2)}) copy-start(f32[2,2,64,384]{2,3,1,0:T(8,128)S(1)} %copy.191) | copy-start | bytes 1179652
  321.7 1.3 copy-start.6
  322.9 128.6 %collective-permute-start.10 = (f32[2,2,384,64]{2,3,1,0:T(8,128)}, f32[2,2,384,64]{2,3,1,0:T(8,128)S(1)}, u32[]{:S(2)}, u32[]{:S(2)}) collective-permute-start(f32[2,2,384,64]{2,3,1,0:T(8,128)} %get-tuple-element.374), channel_id=1, source_target_pairs={{0,1},{1,2},{2,3},{4,5},{5,6},{6,7},{8,9},{9,10},{10,11},{12,13},{... | collective-permute-start | bytes 1179656 | tf_op jit(solution)/shard_map/ppermute | solution.py:21
  326.3 125.2 %collective-permute-start.11 = (f32[2,2,384,64]{2,3,1,0:T(8,128)}, f32[2,2,384,64]{2,3,1,0:T(8,128)}, u32[]{:S(2)}, u32[]{:S(2)}) collective-permute-start(f32[2,2,384,64]{2,3,1,0:T(8,128)} %get-tuple-element.375), channel_id=1, source_target_pairs={{1,0},{2,1},{3,2},{5,4},{6,5},{7,6},{9,8},{10,9},{11,10},{13,12},{... | collective-permute-start | bytes 1179656 | tf_op jit(solution)/shard_map/ppermute | solution.py:22
  (3 other events, 2.7 us)
Sparse Core Ops, SparseCore 0:
  132.1 145.2 all-reduce.6
  317.2 131.0 all-reduce.4
where the time goes:
time: 488 us; the launch traced here: 483 us
  waiting for transfers between devices  285 us (58%)
  local copies, waits for them, and re-layouts  73.1 us (15%)
  starting transfers between devices  36 us (7%)
  other arithmetic  32.3 us (7%)
  matrix products  25.2 us (5%)
  between operations  16.2 us (3%)
  loops' own time  15.5 us (3%)
    psum x2, waiting for transfers between devices, local_pass(): lax.psum((probe_terms, illumination), ('row', 'col'))  262 us
    ppermute x6, starting transfers between devices, extended_2(): before = lax.ppermute(last, axis, up)  28 us
    another operation x2, loops' own time, local_pass(): lax.fori_loop(0, slot_count, place, jnp.zeros(extended.shape, jnp.float32))  14.8 us
    ppermute x6, waiting for transfers between devices, extended_2(): after = lax.ppermute(initial, axis, down)  14.3 us
    dynamic_update_slice x6, local copies, waits for them, and re-layouts, place(): lax.dynamic_update_slice(buffer, present + object_grads[slot_index], start)  13.4 us
    dot_general x12, matrix products, fourier_field(): jnp.einsum('pqab,kmqbc->kmpac', left_table, field, precision=highest)  12.7 us
    dot_general x12, matrix products, fourier_field(): jnp.einsum('kmqab,qpbc->kmpac', upper, right_table, precision=highest)  12.4 us
    unnamed x87, local copies, waits for them, and re-layouts  12 us
  transfers between devices with their start and end apart: 14, of which 8 were waited for; matrix products, arithmetic and copies ran while one was open for 5% of the time, Pallas kernels for 0%

commit v1 on v0

v1 whole, which is shorter than its diff:
```python
import functools
import math

import jax
import jax.numpy as jnp
import ml_dtypes
import numpy as np
from jax import lax
from jax.experimental import pallas as pl
from jax.experimental.pallas import tpu as pltpu
from jax.sharding import PartitionSpec as P

ITERS = 2
VMEM_BYTES = 48 * 1024 * 1024
MESH = pl.DeviceIdType.MESH
DIRS = ((-1, 0), (1, 0), (0, -1), (0, 1), (-1, -1), (-1, 1), (1, -1), (1, 1))


def real_block(table):
    return np.block([[table.real, -table.imag], [table.imag, table.real]])


def transform_tables(width):
    index = np.arange(width)
    product = np.outer(index, index) % width
    far = np.exp(-2j * math.pi * product / width) / math.sqrt(width)
    frequency = (index + width // 2) % width - width // 2
    factor = np.exp(-4j * math.pi * frequency.astype(np.float64) ** 2 / width**2)
    step = far.conj() @ (factor[:, None] * far)
    step = (step + step.T) / 2
    blocks = np.stack([real_block(far), real_block(far).T, real_block(step), real_block(step).T])
    high = blocks.astype(ml_dtypes.bfloat16)
    low = (blocks - high.astype(np.float64)).astype(ml_dtypes.bfloat16)
    return np.stack([high, low], axis=1)


def split_parts(value):
    high = value.astype(jnp.bfloat16)
    return high, (value - high.astype(jnp.float32)).astype(jnp.bfloat16)


def dot(first, second):
    return jnp.dot(first, second, preferred_element_type=jnp.float32)


def apply_transform(tab_ref, left, fields):
    right = left + 1 if left % 2 == 0 else left - 1
    width = fields[0][0].shape[0]
    stacked = jnp.concatenate([jnp.concatenate([r, i], axis=0) for r, i in fields], axis=1)
    high, low = split_parts(stacked)
    t_high, t_low = tab_ref[left, 0], tab_ref[left, 1]
    upper = dot(t_high, high) + dot(t_high, low) + dot(t_low, high)
    rows = []
    for m in range(len(fields)):
        cols = slice(m * width, (m + 1) * width)
        rows.append(jnp.concatenate([upper[:width, cols], upper[width:, cols]], axis=1))
    high, low = split_parts(jnp.concatenate(rows, axis=0))
    t_high, t_low = tab_ref[right, 0], tab_ref[right, 1]
    out = dot(high, t_high) + dot(low, t_high) + dot(high, t_low)
    return [
        (out[m * width : (m + 1) * width, :width], out[m * width : (m + 1) * width, width:])
        for m in range(len(fields))
    ]


def times(a, b):
    return (a[0] * b[0] - a[1] * b[1], a[0] * b[1] + a[1] * b[0])


def conj_times(a, b):
    return (a[0] * b[0] + a[1] * b[1], a[0] * b[1] - a[1] * b[0])


def pass_kernel(
    tile, pos_ref, cnt_ref, center_ref, left_ref, right_ref, modes_ref, meas_ref, tab_ref,
    grad_ref, gl_ref, gr_ref, sums_ref, ext,
):
    tile_rows, tile_cols = tile
    width = meas_ref.shape[-1]
    half = width // 2
    slots = meas_ref.shape[0]
    modes = modes_ref.shape[0] // 2
    last = width + tile_cols
    ext[:, :, width:last] = center_ref[...]
    for q in range(2):
        ext[q, :, :width] = pltpu.roll(left_ref[q], half, 1)
        ext[q + 2, :, :width] = left_ref[q]
        ext[q, :, last:] = right_ref[q]
        ext[q + 2, :, last:] = pltpu.roll(right_ref[q], half, 1)
    grad_ref[...] = jnp.zeros_like(grad_ref)
    sums_ref[...] = jnp.zeros_like(sums_ref)
    row0 = lax.axis_index("row") * tile_rows - half
    col0 = lax.axis_index("col") * tile_cols - width
    lane = lax.broadcasted_iota(jnp.int32, (width, width), 1)
    tall_lane = lax.broadcasted_iota(jnp.int32, (width + 8, width), 1)

    def slot(k, carry):
        @pl.when(k < cnt_ref[0, 0])
        def _():
            row = pos_ref[k, 0] - row0
            col = pos_ref[k, 1] - col0
            base = pl.multiple_of((col // width) * width, width)
            shift = col % width
            top = pl.multiple_of((row // 8) * 8, 8)
            down = row % 8
            up = (width + 8 - down) % (width + 8)
            back_shift = (width - shift) % width

            def cut(p):
                window = ext[p, pl.ds(top, width + 8), pl.ds(base, 2 * width)]
                window = pltpu.roll(window, up, 0)[:width]
                first = pltpu.roll(window[:, :width], back_shift, 1)
                second = pltpu.roll(window[:, width:], back_shift, 1)
                return jnp.where(lane < width - shift, first, second)

            o0 = (cut(0), cut(1))
            o1 = (cut(2), cut(3))
            probe = [(modes_ref[2 * m], modes_ref[2 * m + 1]) for m in range(modes)]
            waves = apply_transform(tab_ref, 2, [times(p, o0) for p in probe])
            far = apply_transform(tab_ref, 0, [times(w, o1) for w in waves])
            intensity = sum(r * r + i * i for r, i in far)
            weight = 2.0 * (intensity - meas_ref[k])
            grads = apply_transform(tab_ref, 1, [(weight * r, weight * i) for r, i in far])

            def add_patch(p, value):
                value = jnp.concatenate([value, jnp.zeros((8, width), jnp.float32)], axis=0)
                rolled = pltpu.roll(pltpu.roll(value, down, 0), shift, 1)
                rows = pl.ds(top, width + 8)
                grad_ref[p, rows, pl.ds(base, width)] += jnp.where(tall_lane >= shift, rolled, 0.0)
                after = pl.multiple_of(base + width, width)
                grad_ref[p, rows, pl.ds(after, width)] += jnp.where(tall_lane < shift, rolled, 0.0)

            terms = [conj_times(w, g) for w, g in zip(waves, grads)]
            add_patch(2, sum(t[0] for t in terms))
            add_patch(3, sum(t[1] for t in terms))
            grads = apply_transform(tab_ref, 3, [conj_times(o1, g) for g in grads])
            terms = [conj_times(p, g) for p, g in zip(probe, grads)]
            add_patch(0, sum(t[0] for t in terms))
            add_patch(1, sum(t[1] for t in terms))
            for m in range(modes):
                back = conj_times(o0, grads[m])
                sums_ref[2 * m] += back[0]
                sums_ref[2 * m + 1] += back[1]
            sums_ref[2 * modes] += o0[0] * o0[0] + o0[1] * o0[1]

        return carry

    lax.fori_loop(0, slots, slot, 0)
    lane = lax.broadcasted_iota(jnp.int32, (grad_ref.shape[1], width), 1)
    for q in range(2):
        gl_ref[q] = jnp.where(
            lane < half, pltpu.roll(grad_ref[q, :, :width], half, 1), grad_ref[q + 2, :, :width]
        )
        gr_ref[q] = jnp.where(
            lane < half, grad_ref[q, :, last:], pltpu.roll(grad_ref[q + 2, :, last:], half, 1)
        )


def local_pass(extended, modes, measured, positions, counts, tables, tile):
    center, left, right = extended
    rows = center.shape[1]
    width = measured.shape[-1]
    wide = center.shape[2] + 2 * width
    smem = pl.BlockSpec(memory_space=pltpu.SMEM)
    vmem = pl.BlockSpec(memory_space=pltpu.VMEM)
    shape = lambda *s: jax.ShapeDtypeStruct(s, jnp.float32)
    return pl.pallas_call(
        functools.partial(pass_kernel, tile),
        out_shape=(
            shape(4, rows, wide),
            shape(2, rows, width),
            shape(2, rows, width),
            shape(modes.shape[0] + 1, width, width),
        ),
        in_specs=[smem, smem] + [vmem] * 6,
        out_specs=(vmem,) * 4,
        scratch_shapes=[pltpu.VMEM((4, rows, wide), jnp.float32)],
        compiler_params=pltpu.CompilerParams(vmem_limit_bytes=VMEM_BYTES),
        name="local_pass",
    )(positions, counts, center, left, right, modes, measured, tables)


class Neighbours:
    def __init__(self, sizes, me, pieces, send_sems, recv_sems):
        self.sizes, self.me, self.pieces = sizes, me, pieces
        self.send_sems, self.recv_sems = send_sems, recv_sems

    def there(self, dr, dc):
        (rows, cols), (r, c) = self.sizes, self.me
        found = None
        for cond in (
            [r > 0] if dr < 0 else [r < rows - 1] if dr > 0 else []
        ) + ([c > 0] if dc < 0 else [c < cols - 1] if dc > 0 else []):
            found = cond if found is None else jnp.logical_and(found, cond)
        return found

    def copy(self, d):
        dr, dc = DIRS[d]
        src, dst = self.pieces[d]
        return pltpu.make_async_remote_copy(
            src_ref=src, dst_ref=dst, send_sem=self.send_sems.at[d], recv_sem=self.recv_sems.at[d],
            device_id=(self.me[0] + dr, self.me[1] + dc), device_id_type=MESH,
        )

    def start(self):
        for d, (dr, dc) in enumerate(DIRS):
            @pl.when(self.there(dr, dc))
            def _(d=d):
                self.copy(d).start()

    def wait_recv(self, after=None):
        for d, (dr, dc) in enumerate(DIRS):
            @pl.when(self.there(-dr, -dc))
            def _(d=d):
                self.copy(d).wait_recv()
                if after is not None:
                    after(d)

    def wait_send(self):
        for d, (dr, dc) in enumerate(DIRS):
            @pl.when(self.there(dr, dc))
            def _(d=d):
                self.copy(d).wait_send()


def reduce_stages(sizes, width):
    stages, size = [], width
    for axis in range(2):
        mask = 1
        while mask < sizes[axis]:
            halves = axis == 0 and size >= 16
            size = size // 2 if halves else size
            stages.append((axis, mask, size, halves))
            mask *= 2
    return stages


def exchange_kernel(sizes, has_sums, has_halo, stages, row_off, *refs):
    refs = list(refs)
    take = lambda n: [refs.pop(0) for _ in range(n)]
    (obj_ref,) = take(1)
    if has_sums:
        grad_ref, gl_ref, gr_ref, sums_ref, modes_ref = take(5)
    if has_halo:
        center_ref, left_ref, right_ref = take(3)
    else:
        (out_ref,) = take(1)
    if has_sums:
        (new_modes_ref,) = take(1)
    if has_halo:
        pack_l, pack_r, halo_send, halo_recv = take(4)
    if has_sums:
        total, from_u, from_d, from_l, from_r, from_ul, from_ur, from_dl, from_dr = take(9)
        rim_send, rim_recv, acc, ar_send, ar_recv, ag_send, ag_recv = take(7)
        landing = refs

    r, c = lax.axis_index("row"), lax.axis_index("col")
    me = (r, c)
    if has_halo:
        tile_rows, tile_cols = center_ref.shape[1] // 2, center_ref.shape[2]
        width = left_ref.shape[-1]
    else:
        tile_rows, tile_cols = out_ref.shape[1], out_ref.shape[2]
        width = gl_ref.shape[-1]
    half = width // 2
    lane = lax.broadcasted_iota(jnp.int32, (tile_rows, width), 1)

    def partner(axis, mask):
        bit = (me[axis] // mask) % 2
        other = me[axis] + mask * (1 - 2 * bit)
        return bit, ((other, c) if axis == 0 else (r, other))

    near = Neighbours(sizes, me, None, None, None)
    barrier = pltpu.get_barrier_semaphore()
    expected = 0
    for dr, dc in DIRS:
        cond = near.there(dr, dc)
        expected = expected + cond.astype(jnp.int32)

        @pl.when(cond)
        def _(dr=dr, dc=dc):
            pl.semaphore_signal(barrier, inc=1, device_id=(r + dr, c + dc), device_id_type=MESH)

    if has_sums:
        for axis, mask, _, _ in stages:
            _, device = partner(axis, mask)
            pl.semaphore_signal(barrier, inc=1, device_id=device, device_id_type=MESH)
            expected = expected + 1
    pl.semaphore_wait(barrier, expected)

    if has_sums:
        top, bottom = slice(0, half), slice(tile_rows + half, tile_rows + width)
        inner = slice(half, tile_rows + half)
        cols = slice(width, width + tile_cols)
        rims = Neighbours(sizes, me, [
            (grad_ref.at[:, top, cols], from_d),
            (grad_ref.at[:, bottom, cols], from_u),
            (gl_ref.at[:, inner, :], from_r),
            (gr_ref.at[:, inner, :], from_l),
            (gl_ref.at[:, top, :], from_dr),
            (gr_ref.at[:, top, :], from_dl),
            (gl_ref.at[:, bottom, :], from_ur),
            (gr_ref.at[:, bottom, :], from_ul),
        ], rim_send, rim_recv)
        rims.start()

        offs = [jnp.int32(0)]
        for axis, mask, size, halves in stages:
            bit, _ = partner(axis, mask)
            offs.append(offs[-1] + bit * size if halves else offs[-1])

        def rows_at(off, size):
            return pl.ds(pl.multiple_of(off, 8), size)

        def reduce_copy(s):
            axis, mask, size, halves = stages[s]
            bit, device = partner(axis, mask)
            sent = offs[s] + (1 - bit) * size if halves else offs[s]
            source = sums_ref if s == 0 else acc
            return pltpu.make_async_remote_copy(
                src_ref=source.at[:, rows_at(sent, size), :], dst_ref=landing[s],
                send_sem=ar_send.at[s], recv_sem=ar_recv.at[s], device_id=device, device_id_type=MESH,
            )

        def reduce_finish(s):
            reduce_copy(s).wait()
            kept = rows_at(offs[s + 1], stages[s][2])
            source = sums_ref if s == 0 else acc
            acc[:, kept, :] = source[:, kept, :] + landing[s][...]

        reduce_copy(0).start()
        reduce_finish(0)
        reduce_copy(1).start()
        total[...] = grad_ref[:, inner, cols]

        def add_rim(d):
            if d == 0:
                total[:, tile_rows - half :, :] += from_d[...]
            elif d == 1:
                total[:, :half, :] += from_u[...]
            else:
                source, rows = {
                    2: (from_r, slice(0, tile_rows)), 3: (from_l, slice(0, tile_rows)),
                    4: (from_dr, slice(tile_rows - half, tile_rows)),
                    5: (from_dl, slice(tile_rows - half, tile_rows)),
                    6: (from_ur, slice(0, half)), 7: (from_ul, slice(0, half)),
                }[d]
                side = lane[rows]
                for q in range(2):
                    value = source[q]
                    turned = pltpu.roll(value, half, 1)
                    if d in (3, 5, 7):
                        total[q, rows, :width] += jnp.where(side < half, value, 0.0)
                        total[q + 2, rows, :width] += jnp.where(side < half, turned, 0.0)
                    else:
                        total[q, rows, tile_cols - width :] += jnp.where(side >= half, turned, 0.0)
                        total[q + 2, rows, tile_cols - width :] += jnp.where(side >= half, value, 0.0)

        rims.wait_recv(add_rim)
        new = obj_ref[:, row_off : row_off + tile_rows, :] - 0.1 * total[...]
    else:
        new = obj_ref[...]

    if has_halo:
        center_ref[:, half : half + tile_rows, :] = new
        for q in range(2):
            lower, upper = new[q], new[q + 2]
            pack_l[q] = jnp.where(lane < half, lower[:, :width], pltpu.roll(upper[:, :width], half, 1))
            pack_r[q] = jnp.where(
                lane < half, pltpu.roll(lower[:, tile_cols - width :], half, 1), upper[:, tile_cols - width :]
            )
        first, final = slice(0, half), slice(tile_rows + half, tile_rows + width)
        middle = slice(half, half + tile_rows)
        ends = slice(tile_rows - half, tile_rows)
        halos = Neighbours(sizes, me, [
            (center_ref.at[:, half:width, :], center_ref.at[:, final, :]),
            (center_ref.at[:, tile_rows : tile_rows + half, :], center_ref.at[:, first, :]),
            (pack_l, right_ref.at[:, middle, :]),
            (pack_r, left_ref.at[:, middle, :]),
            (pack_l.at[:, first, :], right_ref.at[:, final, :]),
            (pack_r.at[:, first, :], left_ref.at[:, final, :]),
            (pack_l.at[:, ends, :], right_ref.at[:, first, :]),
            (pack_r.at[:, ends, :], left_ref.at[:, first, :]),
        ], halo_send, halo_recv)
        halos.start()
    else:
        out_ref[...] = new

    if has_sums:
        reduce_finish(1)
        for s in range(2, len(stages)):
            reduce_copy(s).start()
            reduce_finish(s)
        planes = modes_ref.shape[0]
        kept = rows_at(offs[-1], stages[-1][2])
        scale = 0.25 / jnp.sqrt(acc[planes, kept, :])
        new_modes_ref[:, kept, :] = modes_ref[:, kept, :] - acc[:planes, kept, :] * scale[None]
        for s in reversed(range(len(stages))):
            axis, mask, size, halves = stages[s]
            if halves:
                _, device = partner(axis, mask)
                part = new_modes_ref.at[:, rows_at(offs[s + 1], size), :]
                copy = pltpu.make_async_remote_copy(
                    src_ref=part, dst_ref=part, send_sem=ag_send.at[s], recv_sem=ag_recv.at[s],
                    device_id=device, device_id_type=MESH,
                )
                copy.start()
                copy.wait()
        rims.wait_send()
    if has_halo:
        halos.wait_recv()
        halos.wait_send()


def exchange(sizes, tile, width, ident, obj, sums=None, halo=True, row_off=0):
    tile_rows, tile_cols = tile
    half = width // 2
    rows = tile_rows + width
    vmem = pl.BlockSpec(memory_space=pltpu.VMEM)
    shape = lambda *s: jax.ShapeDtypeStruct(s, jnp.float32)
    buf = lambda *s: pltpu.VMEM(s, jnp.float32)
    dma = lambda n: pltpu.SemaphoreType.DMA((n,))
    operands, outs, scratch, stages = [obj], [], [], []
    if halo:
        outs += [shape(4, rows, tile_cols), shape(2, rows, width), shape(2, rows, width)]
        scratch += [buf(2, tile_rows, width), buf(2, tile_rows, width), dma(8), dma(8)]
    else:
        outs += [shape(4, tile_rows, tile_cols)]
    if sums is not None:
        operands += list(sums)
        planes = sums[-1].shape[0]
        outs += [shape(planes, width, width)]
        stages = reduce_stages(sizes, width)
        scratch += [
            buf(4, tile_rows, tile_cols),
            buf(4, half, tile_cols), buf(4, half, tile_cols),
            buf(2, tile_rows, width), buf(2, tile_rows, width),
            buf(2, half, width), buf(2, half, width), buf(2, half, width), buf(2, half, width),
            dma(8), dma(8),
            buf(planes + 1, width, width),
            dma(len(stages)), dma(len(stages)), dma(len(stages)), dma(len(stages)),
        ] + [buf(planes + 1, size, width) for _, _, size, _ in stages]
    return pl.pallas_call(
        functools.partial(exchange_kernel, sizes, sums is not None, halo, stages, row_off),
        out_shape=tuple(outs),
        in_specs=[vmem] * len(operands),
        out_specs=(vmem,) * len(outs),
        scratch_shapes=scratch,
        compiler_params=pltpu.CompilerParams(
            collective_id=ident, has_side_effects=True, vmem_limit_bytes=VMEM_BYTES
        ),
        name="exchange_%d" % ident,
    )(*operands)


def body(sizes, objects, probe_modes, intensities, positions, counts):
    width = probe_modes.shape[-1]
    tile = objects.shape[2:]
    modes = probe_modes.reshape(-1, width, width)
    tables = jnp.asarray(transform_tables(width))
    objects4 = objects.reshape((4,) + tile)
    extended = exchange(sizes, tile, width, 0, objects4)
    for step in range(ITERS):
        final = step == ITERS - 1
        sums = local_pass(extended, modes, intensities[0, 0], positions[0, 0], counts, tables, tile)
        result = exchange(
            sizes, tile, width, step + 1, extended[0], tuple(sums) + (modes,),
            halo=not final, row_off=width // 2,
        )
        modes = result[-1]
        extended = result[:-1]
    return extended[0].reshape(objects.shape), modes.reshape(probe_modes.shape)


def solution(mesh):
    sizes = (mesh.shape["row"], mesh.shape["col"])
    return jax.shard_map(
        functools.partial(body, sizes),
        mesh=mesh,
        in_specs=(
            P(None, None, "row", "col"),
            P(),
            P("row", "col", None, None, None),
            P("row", "col", None, None),
            P("row", "col"),
        ),
        out_specs=(P(None, None, "row", "col"), P()),
        check_vma=False,
    )
```

time: 488 us -> 119 us (0.24)
  waiting for transfers between devices: 285 us -> 0 us
  Pallas kernels: 0 us -> 110 us
  local copies, waits for them, and re-layouts: 73.1 us -> 8.07 us
  starting transfers between devices: 36 us -> 0 us
  other arithmetic: 32.3 us -> 0 us
  matrix products: 25.2 us -> 0 us
  loops' own time: 15.5 us -> 0 us
  between operations: 16.2 us -> 1.4 us
    psum x2 -> x0, waiting for transfers between devices: 262 us -> none  [local_pass(): lax.psum((probe_terms, illumination), ('row', 'col'))]
    pallas_call x0 -> x5, Pallas kernels: none -> 110 us  [the longest x3 97.1 us: exchange(): pl.pallas_call(functools.partial(exchange_kernel, sizes, sums is not None...]
    ppermute x12 -> x0, starting transfers between devices: 35.7 us -> none  [the longest x6 28 us: extended_2(): before = lax.ppermute(last, axis, up)]
    dot_general x24 -> x0, matrix products: 25.2 us -> none  [the longest x12 12.7 us: fourier_field(): jnp.einsum('pqab,kmqbc->kmpac', left_table, field, precision=highest)]
    ppermute x12 -> x0, waiting for transfers between devices: 23.5 us -> none  [the longest x6 14.3 us: extended_2(): after = lax.ppermute(initial, axis, down)]
    another operation x4 -> x0, loops' own time: 15.5 us -> none  [the longest x2 14.8 us: local_pass(): lax.fori_loop(0, slot_count, place, jnp.zeros(extended.shape, jnp.float32))]
    dynamic_update_slice x6 -> x0, local copies, waits for them, and re-layouts: 13.4 us -> none  [place(): lax.dynamic_update_slice(buffer, present + object_grads[slot_index], start)]
    scatter-add x2 -> x0, local copies, waits for them, and re-layouts: 11.4 us -> none  [the longest x1 6.12 us: fold_rims(): middle.at[:, :, inner_rows - margin:, :]]
  transfers between devices with their start and end apart: 14 -> 0, of which waited for: 8 -> 0; matrix products, arithmetic and copies ran while one was open for 5% -> 0% of each run, Pallas kernels for 0% -> 0%
where the time goes in v1:
time: 119 us
  Pallas kernels  110 us (92%)
  local copies, waits for them, and re-layouts  8.07 us (7%)
  between operations  1.4 us (1%)
    pallas_call x3, Pallas kernels, exchange(): pl.pallas_call(functools.partial(exchange_kernel, sizes, sums is not None...  97.1 us
    pallas_call x2, Pallas kernels, local_pass(): pl.pallas_call(functools.partial(pass_kernel, tile), out_shape=(shape(4,...  12.6 us
    unnamed x18, local copies, waits for them, and re-layouts  8.07 us

profile of v1, /device:TPU:0, one launch (start us, length us, event | category | flops | bytes accessed | tf_op | source)
XLA Modules:
  0.0 119.2 jit_solution(4548273584383007653)
XLA Ops:
  0.6 0.0 copy-start.3
  1.3 0.0 copy-start.6
  1.4 1.0 copy-done.6
  2.4 10.7 %exchange_0.1 = (f32[4,256,256]{2,1,0:T(8,128)S(1)}, f32[2,256,128]{2,1,0:T(8,128)S(1)}, f32[2,256,128]{2,1,0:T(8,128)S(1)}) custom-call(f32[4,128,256]{2,1,0:T(8,128)S(1)} %bitcast.10), custom_call_target="tpu_custom_call" | custom-call | tf_op jit(solution)/shard_map/exchange_0/pallas_call | solution.py:443
  13.1 0.0 copy-start
  13.1 1.2 %copy-done = bf16[4,2,256,256]{3,2,1,0:T(8,128)(2,1)S(1)} copy-done((bf16[4,2,256,256]{3,2,1,0:T(8,128)(2,1)S(1)}, bf16[4,2,256,256]{3,2,1,0:T(8,128)(2,1)}, u32[]{:S(2)}) %copy-start) | copy-done | bytes 1048600
  14.3 0.0 copy-start.2
  14.3 1.0 copy-done.2
  15.3 0.0 copy-start.5
  15.3 0.9 copy-done.5
  16.2 0.0 copy-start.7
  16.2 0.7 copy-done.7
  16.9 6.3 %local_pass.2 = (f32[4,256,512]{2,1,0:T(8,128)}, f32[2,256,128]{2,1,0:T(8,128)S(1)}, f32[2,256,128]{2,1,0:T(8,128)S(1)}, f32[9,128,128]{2,1,0:T(8,128)S(1)}) custom-call(s32[2,2]{1,0:T(2,128)S(1)} %bitcast.13, s32[1,1]{1,0:T(1,128)S(6)} %copy.10.cnt_ref, f32[4,256,256]{2,1,0:T(8,128)S(1)} %get-tuple-element.19.center_ref.refs_0_, ...), custom_call_target="tpu_custom_call" | custom-call | tf_op jit(solution)/shard_map/local_pass/pallas_call | solution.py:167
  23.2 0.0 copy-done.3
  23.2 0.0 copy-start.1
  23.2 47.4 %exchange_1.1 = (f32[4,256,256]{2,1,0:T(8,128)S(1)}, f32[2,256,128]{2,1,0:T(8,128)S(1)}, f32[2,256,128]{2,1,0:T(8,128)S(1)}, f32[8,128,128]{2,1,0:T(8,128)S(1)}) custom-call(f32[4,256,256]{2,1,0:T(8,128)S(1)} %get-tuple-element.19.center_ref.refs_0_, f32[4,256,512]{2,1,0:T(8,128)} %get-tuple-element.22.refs_1_, ...), custom_call_target="tpu_custom_call" | custom-call | tf_op jit(solution)/shard_map/exchange_1/pallas_call | solution.py:443
  70.6 0.0 copy-done.1
  70.6 6.3 %local_pass.3 = (f32[4,256,512]{2,1,0:T(8,128)}, f32[2,256,128]{2,1,0:T(8,128)S(1)}, f32[2,256,128]{2,1,0:T(8,128)S(1)}, f32[9,128,128]{2,1,0:T(8,128)S(1)}) custom-call(s32[2,2]{1,0:T(2,128)S(1)} %bitcast.14, s32[1,1]{1,0:T(1,128)S(6)} %copy.10.cnt_ref, f32[4,256,256]{2,1,0:T(8,128)S(1)} %get-tuple-element.26.center_ref.refs_0_, ...), custom_call_target="tpu_custom_call" | custom-call | tf_op jit(solution)/shard_map/local_pass/pallas_call | solution.py:167
  76.9 0.0 copy-start.4
  76.9 1.6 %copy-done.4 = f32[4,256,512]{2,1,0:T(8,128)S(1)} copy-done((f32[4,256,512]{2,1,0:T(8,128)S(1)}, f32[4,256,512]{2,1,0:T(8,128)}, u32[]{:S(2)}) %copy-start.4) | copy-done | bytes 2097176
  78.5 39.1 %exchange_2.1 = (f32[4,128,256]{2,1,0:T(8,128)S(1)}, f32[8,128,128]{2,1,0:T(8,128)S(1)}) custom-call(f32[4,256,256]{2,1,0:T(8,128)S(1)} %get-tuple-element.26.center_ref.refs_0_, f32[4,256,512]{2,1,0:T(8,128)S(1)} %copy-done.4, f32[2,256,128]{2,1,0:T(8,128)S(1)} %get-tuple-element.31.refs_2_, f32[2,256,128]{2,1,0:T(8,128)S(1)} %get-tuple-element.32.refs_3_, ...), custom_call_target="tpu_custom_call" | custom-call | tf_op jit(solution)/shard_map/exchange_2/pallas_call | solution.py:443
  117.6 0.8 copy.11
  118.4 0.8 copy.12
Async XLA Ops:
  0.6 22.6 %copy-start.3 = (f32[4,2,128,128]{3,2,1,0:T(8,128)S(1)}, f32[4,2,128,128]{3,2,1,0:T(8,128)}, u32[]{:S(2)}) copy-start(f32[4,2,128,128]{3,2,1,0:T(8,128)} %param.7) | copy-start | bytes 1572868
  1.3 1.0 copy-start.6
  13.1 1.2 %copy-start = (bf16[4,2,256,256]{3,2,1,0:T(8,128)(2,1)S(1)}, bf16[4,2,256,256]{3,2,1,0:T(8,128)(2,1)}, u32[]{:S(2)}) copy-start(bf16[4,2,256,256]{3,2,1,0:T(8,128)(2,1)} %constant.2.clone.tab_ref) | copy-start | bytes 3145732
  14.3 1.0 copy-start.2
  15.3 0.9 copy-start.5
  16.2 0.7 copy-start.7
  23.2 47.4 %copy-start.1 = (bf16[4,2,256,256]{3,2,1,0:T(8,128)(2,1)S(1)}, bf16[4,2,256,256]{3,2,1,0:T(8,128)(2,1)}, u32[]{:S(2)}) copy-start(bf16[4,2,256,256]{3,2,1,0:T(8,128)(2,1)} %constant.2.clone.tab_ref) | copy-start | bytes 3145732
  76.9 1.6 %copy-start.4 = (f32[4,256,512]{2,1,0:T(8,128)S(1)}, f32[4,256,512]{2,1,0:T(8,128)}, u32[]{:S(2)}) copy-start(f32[4,256,512]{2,1,0:T(8,128)} %get-tuple-element.30.refs_1_) | copy-start | bytes 6291460

commit v2 on v1

--- a/solution.py
+++ b/solution.py
@@ -11,7 +11,8 @@
 from jax.sharding import PartitionSpec as P
 
 ITERS = 2
-VMEM_BYTES = 48 * 1024 * 1024
+PASS_BYTES = 32 * 1024 * 1024
+EXCHANGE_BYTES = 24 * 1024 * 1024
 MESH = pl.DeviceIdType.MESH
 DIRS = ((-1, 0), (1, 0), (0, -1), (0, 1), (-1, -1), (-1, 1), (1, -1), (1, 1))
 
@@ -29,9 +30,11 @@
     step = far.conj() @ (factor[:, None] * far)
     step = (step + step.T) / 2
     blocks = np.stack([real_block(far), real_block(far).T, real_block(step), real_block(step).T])
-    high = blocks.astype(ml_dtypes.bfloat16)
-    low = (blocks - high.astype(np.float64)).astype(ml_dtypes.bfloat16)
-    return np.stack([high, low], axis=1)
+    parts = []
+    for _ in range(3):
+        parts.append(blocks.astype(ml_dtypes.bfloat16))
+        blocks = blocks - parts[-1].astype(np.float64)
+    return np.stack(parts, axis=1)
 
 
 def split_parts(value):
@@ -43,20 +46,27 @@
     return jnp.dot(first, second, preferred_element_type=jnp.float32)
 
 
-def apply_transform(tab_ref, left, fields):
+def products(tab_ref, place, value, table_first, exact):
+    high, low = split_parts(value)
+    pairs = [(0, high), (0, low), (1, high)] + ([(2, high)] if exact else [])
+    total = None
+    for part, operand in pairs:
+        table = tab_ref[place, part]
+        term = dot(table, operand) if table_first else dot(operand, table)
+        total = term if total is None else total + term
+    return total
+
+
+def apply_transform(tab_ref, left, fields, exact):
     right = left + 1 if left % 2 == 0 else left - 1
     width = fields[0][0].shape[0]
     stacked = jnp.concatenate([jnp.concatenate([r, i], axis=0) for r, i in fields], axis=1)
-    high, low = split_parts(stacked)
-    t_high, t_low = tab_ref[left, 0], tab_ref[left, 1]
-    upper = dot(t_high, high) + dot(t_high, low) + dot(t_low, high)
+    upper = products(tab_ref, left, stacked, True, exact)
     rows = []
     for m in range(len(fields)):
         cols = slice(m * width, (m + 1) * width)
         rows.append(jnp.concatenate([upper[:width, cols], upper[width:, cols]], axis=1))
-    high, low = split_parts(jnp.concatenate(rows, axis=0))
-    t_high, t_low = tab_ref[right, 0], tab_ref[right, 1]
-    out = dot(high, t_high) + dot(low, t_high) + dot(high, t_low)
+    out = products(tab_ref, right, jnp.concatenate(rows, axis=0), False, exact)
     return [
         (out[m * width : (m + 1) * width, :width], out[m * width : (m + 1) * width, width:])
         for m in range(len(fields))
@@ -72,7 +82,7 @@
 
 
 def pass_kernel(
-    tile, pos_ref, cnt_ref, center_ref, left_ref, right_ref, modes_ref, meas_ref, tab_ref,
+    tile, exact, pos_ref, cnt_ref, center_ref, left_ref, right_ref, modes_ref, meas_ref, tab_ref,
     grad_ref, gl_ref, gr_ref, sums_ref, ext,
 ):
     tile_rows, tile_cols = tile
@@ -116,11 +126,11 @@
             o0 = (cut(0), cut(1))
             o1 = (cut(2), cut(3))
             probe = [(modes_ref[2 * m], modes_ref[2 * m + 1]) for m in range(modes)]
-            waves = apply_transform(tab_ref, 2, [times(p, o0) for p in probe])
-            far = apply_transform(tab_ref, 0, [times(w, o1) for w in waves])
+            waves = apply_transform(tab_ref, 2, [times(p, o0) for p in probe], exact)
+            far = apply_transform(tab_ref, 0, [times(w, o1) for w in waves], exact)
             intensity = sum(r * r + i * i for r, i in far)
             weight = 2.0 * (intensity - meas_ref[k])
-            grads = apply_transform(tab_ref, 1, [(weight * r, weight * i) for r, i in far])
+            grads = apply_transform(tab_ref, 1, [(weight * r, weight * i) for r, i in far], exact)
 
             def add_patch(p, value):
                 value = jnp.concatenate([value, jnp.zeros((8, width), jnp.float32)], axis=0)
@@ -133,7 +143,7 @@
             terms = [conj_times(w, g) for w, g in zip(waves, grads)]
             add_patch(2, sum(t[0] for t in terms))
             add_patch(3, sum(t[1] for t in terms))
-            grads = apply_transform(tab_ref, 3, [conj_times(o1, g) for g in grads])
+            grads = apply_transform(tab_ref, 3, [conj_times(o1, g) for g in grads], exact)
             terms = [conj_times(p, g) for p, g in zip(probe, grads)]
             add_patch(0, sum(t[0] for t in terms))
             add_patch(1, sum(t[1] for t in terms))
@@ -156,7 +166,7 @@
         )
 
 
-def local_pass(extended, modes, measured, positions, counts, tables, tile):
+def local_pass(extended, modes, measured, positions, counts, tables, tile, exact):
     center, left, right = extended
     rows = center.shape[1]
     width = measured.shape[-1]
@@ -165,7 +175,7 @@
     vmem = pl.BlockSpec(memory_space=pltpu.VMEM)
     shape = lambda *s: jax.ShapeDtypeStruct(s, jnp.float32)
     return pl.pallas_call(
-        functools.partial(pass_kernel, tile),
+        functools.partial(pass_kernel, tile, exact),
         out_shape=(
             shape(4, rows, wide),
             shape(2, rows, width),
@@ -175,7 +185,7 @@
         in_specs=[smem, smem] + [vmem] * 6,
         out_specs=(vmem,) * 4,
         scratch_shapes=[pltpu.VMEM((4, rows, wide), jnp.float32)],
-        compiler_params=pltpu.CompilerParams(vmem_limit_bytes=VMEM_BYTES),
+        compiler_params=pltpu.CompilerParams(vmem_limit_bytes=PASS_BYTES),
         name="local_pass",
     )(positions, counts, center, left, right, modes, measured, tables)
 
@@ -223,16 +233,143 @@
                 self.copy(d).wait_send()
 
 
-def reduce_stages(sizes, width):
-    stages, size = [], width
+def reduce_stages(sizes, width, planes, col_early):
+    groups = [[], []]
     for axis in range(2):
-        mask = 1
-        while mask < sizes[axis]:
-            halves = axis == 0 and size >= 16
-            size = size // 2 if halves else size
-            stages.append((axis, mask, size, halves))
-            mask *= 2
+        mask, left = 1, sizes[axis]
+        while left > 1:
+            radix = 4 if left % 4 == 0 and not (axis == 0 and mask == 1) else 2
+            groups[axis].append((axis, mask, radix))
+            mask, left = mask * radix, left // radix
+    first = 1 if col_early else len(groups[0])
+    stages, rows = [], width
+    for axis, mask, radix in groups[0][:first] + groups[1] + groups[0][first:]:
+        kind = "full"
+        if axis == 0 and rows % (8 * radix) == 0:
+            kind, rows = "rows", rows // radix
+        elif axis == 1 and planes % radix == 0:
+            kind, planes = "planes", planes // radix
+        stages.append((axis, mask, radix, kind, rows, planes))
     return stages
+
+
+def held_shape(stages, s, width, light):
+    _, _, _, _, rows, planes = stages[s]
+    if s + 1 < len(stages) and stages[s + 1][3] == "planes":
+        radix = stages[s + 1][2]
+        return (radix, planes // radix + light, rows, width)
+    return (planes + light, rows, width)
+
+
+class ProbeSum:
+    def __init__(self, me, stages, sums_ref, light, scale_ref, modes_ref, new_ref, landing, held, sems):
+        self.me, self.stages, self.light, self.scale_ref = me, stages, light, scale_ref
+        self.modes_ref, self.new_ref = modes_ref, new_ref
+        self.landing, self.held = landing, [sums_ref] + list(held)
+        self.send_sem, self.recv_sem, self.spread_send, self.spread_recv = sems
+        self.digits, self.where, self.pending = [], [(jnp.int32(0), jnp.int32(0))], []
+        for axis, mask, radix, kind, rows, planes in stages:
+            digit = (me[axis] // mask) % radix
+            row_off, plane_off = self.where[-1]
+            if kind == "rows":
+                row_off = row_off + digit * rows
+            elif kind == "planes":
+                plane_off = plane_off + digit * planes
+            self.digits.append(digit)
+            self.where.append((row_off, plane_off))
+
+    def partner(self, s, j):
+        axis, mask, radix = self.stages[s][:3]
+        other = (self.digits[s] + j) % radix
+        place = self.me[axis] + mask * (other - self.digits[s])
+        return other, ((place, self.me[1]) if axis == 0 else (self.me[0], place))
+
+    def piece(self, s, digit):
+        kind, rows = self.stages[s][3:5]
+        source = self.held[s]
+        if kind == "rows":
+            return source.at[:, pl.ds(pl.multiple_of(digit * rows, 8), rows), :]
+        return source.at[digit] if kind == "planes" else source
+
+    def copy(self, s, j):
+        kind = self.stages[s][3]
+        other, device = self.partner(s, j)
+        slot = self.digits[s] if kind == "full" else j - 1
+        return pltpu.make_async_remote_copy(
+            src_ref=self.piece(s, other), dst_ref=self.landing[s].at[slot],
+            send_sem=self.send_sem.at[s, j - 1], recv_sem=self.recv_sem.at[s, j - 1],
+            device_id=device, device_id_type=MESH,
+        )
+
+    def start(self, s):
+        for j in range(1, self.stages[s][2]):
+            copy = self.copy(s, j)
+            copy.start()
+            self.pending.append(copy)
+
+    def finish(self, s):
+        _, _, radix, kind, _, planes = self.stages[s]
+        own = self.piece(s, self.digits[s])[...]
+        landing = self.landing[s]
+        if kind == "full":
+            landing[self.digits[s]] = own
+        for j in range(1, radix):
+            self.copy(s, j).wait_recv()
+        if kind == "full":
+            value = sum(landing[i] for i in range(radix))
+        else:
+            value = own + sum(landing[i] for i in range(radix - 1))
+        target = self.held[s + 1]
+        if s + 1 < len(self.stages) and self.stages[s + 1][3] == "planes":
+            groups = self.stages[s + 1][2]
+            each = planes // groups
+            for g in range(groups):
+                target[g, :each] = value[g * each : (g + 1) * each]
+                if self.light:
+                    target[g, each] = value[planes]
+        else:
+            target[...] = value
+
+    def region(self, s):
+        row_off, plane_off = self.where[s + 1]
+        rows, planes = self.stages[s][4:]
+        return pl.ds(plane_off, planes), pl.ds(pl.multiple_of(row_off, 8), rows), slice(None)
+
+    def update(self):
+        final = len(self.stages) - 1
+        value = self.held[-1]
+        planes = self.stages[final][5]
+        place = self.region(final)
+        if self.light:
+            self.scale_ref[...] = 0.25 / jnp.sqrt(value[planes])
+        self.new_ref[place] = self.modes_ref[place] - value[:planes] * self.scale_ref[...][None]
+
+    def spread_stages(self):
+        return [s for s in reversed(range(len(self.stages))) if self.stages[s][3] != "full"]
+
+    def spread_copies(self, s):
+        part = self.new_ref.at[self.region(s)]
+        return [
+            pltpu.make_async_remote_copy(
+                src_ref=part, dst_ref=part, send_sem=self.spread_send.at[s, j - 1],
+                recv_sem=self.spread_recv.at[s, j - 1], device_id=self.partner(s, j)[1], device_id_type=MESH,
+            )
+            for j in range(1, self.stages[s][2])
+        ]
+
+    def spread_start(self, s):
+        copies = self.spread_copies(s)
+        for copy in copies:
+            copy.start()
+        self.pending += copies
+
+    def spread_finish(self, s):
+        for copy in self.spread_copies(s):
+            copy.wait_recv()
+
+    def drain(self):
+        for copy in self.pending:
+            copy.wait_send()
 
 
 def exchange_kernel(sizes, has_sums, has_halo, stages, row_off, *refs):
@@ -251,8 +388,9 @@
         pack_l, pack_r, halo_send, halo_recv = take(4)
     if has_sums:
         total, from_u, from_d, from_l, from_r, from_ul, from_ur, from_dl, from_dr = take(9)
-        rim_send, rim_recv, acc, ar_send, ar_recv, ag_send, ag_recv = take(7)
-        landing = refs
+        rim_send, rim_recv = take(2)
+        (scale_ref,) = take(1)
+        scratch = [(take(4), take(len(part)), take(len(part))) for part in stages]
 
     r, c = lax.axis_index("row"), lax.axis_index("col")
     me = (r, c)
@@ -265,11 +403,6 @@
     half = width // 2
     lane = lax.broadcasted_iota(jnp.int32, (tile_rows, width), 1)
 
-    def partner(axis, mask):
-        bit = (me[axis] // mask) % 2
-        other = me[axis] + mask * (1 - 2 * bit)
-        return bit, ((other, c) if axis == 0 else (r, other))
-
     near = Neighbours(sizes, me, None, None, None)
     barrier = pltpu.get_barrier_semaphore()
     expected = 0
@@ -282,10 +415,21 @@
             pl.semaphore_signal(barrier, inc=1, device_id=(r + dr, c + dc), device_id_type=MESH)
 
     if has_sums:
-        for axis, mask, _, _ in stages:
-            _, device = partner(axis, mask)
-            pl.semaphore_signal(barrier, inc=1, device_id=device, device_id_type=MESH)
-            expected = expected + 1
+        planes = modes_ref.shape[0]
+        cut = planes // 2
+        parts = []
+        for part, first, last in ((0, cut, planes), (1, 0, cut)):
+            sems, landing, held = scratch[part]
+            light = 1 - part
+            parts.append(ProbeSum(
+                me, stages[part], sums_ref.at[first : last + light], light, scale_ref,
+                modes_ref.at[first:last], new_modes_ref.at[first:last], landing, held, sems,
+            ))
+        for s in range(len(stages[0])):
+            for j in range(1, stages[0][s][2]):
+                _, device = parts[0].partner(s, j)
+                pl.semaphore_signal(barrier, inc=1, device_id=device, device_id_type=MESH)
+                expected = expected + 1
     pl.semaphore_wait(barrier, expected)
 
     if has_sums:
@@ -302,35 +446,17 @@
             (gl_ref.at[:, bottom, :], from_ur),
             (gr_ref.at[:, bottom, :], from_ul),
         ], rim_send, rim_recv)
-        rims.start()
-
-        offs = [jnp.int32(0)]
-        for axis, mask, size, halves in stages:
-            bit, _ = partner(axis, mask)
-            offs.append(offs[-1] + bit * size if halves else offs[-1])
-
-        def rows_at(off, size):
-            return pl.ds(pl.multiple_of(off, 8), size)
-
-        def reduce_copy(s):
-            axis, mask, size, halves = stages[s]
-            bit, device = partner(axis, mask)
-            sent = offs[s] + (1 - bit) * size if halves else offs[s]
-            source = sums_ref if s == 0 else acc
-            return pltpu.make_async_remote_copy(
-                src_ref=source.at[:, rows_at(sent, size), :], dst_ref=landing[s],
-                send_sem=ar_send.at[s], recv_sem=ar_recv.at[s], device_id=device, device_id_type=MESH,
-            )
-
-        def reduce_finish(s):
-            reduce_copy(s).wait()
-            kept = rows_at(offs[s + 1], stages[s][2])
-            source = sums_ref if s == 0 else acc
-            acc[:, kept, :] = source[:, kept, :] + landing[s][...]
-
-        reduce_copy(0).start()
-        reduce_finish(0)
-        reduce_copy(1).start()
+        count = len(stages[0])
+        if has_halo:
+            rims.start()
+        for part in parts:
+            part.start(0)
+        for part in parts:
+            part.finish(0)
+            if count > 1:
+                part.start(1)
+        if not has_halo:
+            rims.start()
         total[...] = grad_ref[:, inner, cols]
 
         def add_rim(d):
@@ -356,6 +482,27 @@
                         total[q, rows, tile_cols - width :] += jnp.where(side >= half, turned, 0.0)
                         total[q + 2, rows, tile_cols - width :] += jnp.where(side >= half, value, 0.0)
 
+        def reduce_step(s):
+            for part in parts:
+                part.finish(s)
+                if s + 1 < count:
+                    part.start(s + 1)
+
+        def spread_step(n):
+            for part, order in zip(parts, orders):
+                if n == 0:
+                    part.update()
+                else:
+                    part.spread_finish(order[n - 1])
+                if n < len(order):
+                    part.spread_start(order[n])
+
+        orders = [part.spread_stages() for part in parts]
+        early = 2 if has_halo else count
+        for s in range(1, early):
+            reduce_step(s)
+        if not has_halo:
+            spread_step(0)
         rims.wait_recv(add_rim)
         new = obj_ref[:, row_off : row_off + tile_rows, :] - 0.1 * total[...]
     else:
@@ -387,25 +534,12 @@
         out_ref[...] = new
 
     if has_sums:
-        reduce_finish(1)
-        for s in range(2, len(stages)):
-            reduce_copy(s).start()
-            reduce_finish(s)
-        planes = modes_ref.shape[0]
-        kept = rows_at(offs[-1], stages[-1][2])
-        scale = 0.25 / jnp.sqrt(acc[planes, kept, :])
-        new_modes_ref[:, kept, :] = modes_ref[:, kept, :] - acc[:planes, kept, :] * scale[None]
-        for s in reversed(range(len(stages))):
-            axis, mask, size, halves = stages[s]
-            if halves:
-                _, device = partner(axis, mask)
-                part = new_modes_ref.at[:, rows_at(offs[s + 1], size), :]
-                copy = pltpu.make_async_remote_copy(
-                    src_ref=part, dst_ref=part, send_sem=ag_send.at[s], recv_sem=ag_recv.at[s],
-                    device_id=device, device_id_type=MESH,
-                )
-                copy.start()
-                copy.wait()
+        for s in range(early, count):
+            reduce_step(s)
+        for n in range(0 if has_halo else 1, len(orders[0]) + 1):
+            spread_step(n)
+        for part in parts:
+            part.drain()
         rims.wait_send()
     if has_halo:
         halos.wait_recv()
@@ -419,36 +553,44 @@
     vmem = pl.BlockSpec(memory_space=pltpu.VMEM)
     shape = lambda *s: jax.ShapeDtypeStruct(s, jnp.float32)
     buf = lambda *s: pltpu.VMEM(s, jnp.float32)
-    dma = lambda n: pltpu.SemaphoreType.DMA((n,))
+    dma = lambda *n: pltpu.SemaphoreType.DMA(n)
     operands, outs, scratch, stages = [obj], [], [], []
+    specs = [vmem]
     if halo:
         outs += [shape(4, rows, tile_cols), shape(2, rows, width), shape(2, rows, width)]
-        scratch += [buf(2, tile_rows, width), buf(2, tile_rows, width), dma(8), dma(8)]
     else:
         outs += [shape(4, tile_rows, tile_cols)]
+    if halo:
+        scratch += [buf(2, tile_rows, width), buf(2, tile_rows, width), dma(8), dma(8)]
     if sums is not None:
         operands += list(sums)
+        specs += [vmem] * len(sums)
         planes = sums[-1].shape[0]
         outs += [shape(planes, width, width)]
-        stages = reduce_stages(sizes, width)
+        stages = [reduce_stages(sizes, width, planes // 2, col_early) for col_early in (False, True)]
         scratch += [
             buf(4, tile_rows, tile_cols),
             buf(4, half, tile_cols), buf(4, half, tile_cols),
             buf(2, tile_rows, width), buf(2, tile_rows, width),
             buf(2, half, width), buf(2, half, width), buf(2, half, width), buf(2, half, width),
-            dma(8), dma(8),
-            buf(planes + 1, width, width),
-            dma(len(stages)), dma(len(stages)), dma(len(stages)), dma(len(stages)),
-        ] + [buf(planes + 1, size, width) for _, _, size, _ in stages]
+            dma(8), dma(8), buf(stages[0][-1][4], width),
+        ]
+        for part, light in zip(stages, (1, 0)):
+            scratch += [dma(len(part), 3) for _ in range(4)]
+            for _, _, radix, kind, rows_held, planes_held in part:
+                slots = radix if kind == "full" else radix - 1
+                scratch.append(buf(slots, planes_held + light, rows_held, width))
+            scratch += [buf(*held_shape(part, s, width, light)) for s in range(len(part))]
     return pl.pallas_call(
         functools.partial(exchange_kernel, sizes, sums is not None, halo, stages, row_off),
         out_shape=tuple(outs),
-        in_specs=[vmem] * len(operands),
+        in_specs=specs,
         out_specs=(vmem,) * len(outs),
         scratch_shapes=scratch,
         compiler_params=pltpu.CompilerParams(
-            collective_id=ident, has_side_effects=True, vmem_limit_bytes=VMEM_BYTES
+            collective_id=ident, has_side_effects=True, vmem_limit_bytes=EXCHANGE_BYTES
         ),
+        cost_estimate=pl.CostEstimate(flops=0, transcendentals=0, bytes_accessed=32 * 1024 * 1024),
         name="exchange_%d" % ident,
     )(*operands)
 
@@ -456,13 +598,15 @@
 def body(sizes, objects, probe_modes, intensities, positions, counts):
     width = probe_modes.shape[-1]
     tile = objects.shape[2:]
+    tables = jnp.asarray(transform_tables(width))
     modes = probe_modes.reshape(-1, width, width)
-    tables = jnp.asarray(transform_tables(width))
-    objects4 = objects.reshape((4,) + tile)
-    extended = exchange(sizes, tile, width, 0, objects4)
+    measured = intensities[0, 0]
+    extended = exchange(sizes, tile, width, 0, objects.reshape((4,) + tile))
     for step in range(ITERS):
         final = step == ITERS - 1
-        sums = local_pass(extended, modes, intensities[0, 0], positions[0, 0], counts, tables, tile)
+        sums = local_pass(
+            extended, modes, measured, positions[0, 0], counts, tables, tile, exact=not final
+        )
         result = exchange(
             sizes, tile, width, step + 1, extended[0], tuple(sums) + (modes,),
             halo=not final, row_off=width // 2,

time: 119 us -> 101 us (0.85)
  Pallas kernels: 110 us -> 92.4 us
  local copies, waits for them, and re-layouts: 8.07 us -> 6.67 us
    pallas_call x2, Pallas kernels: 12.6 us -> 2.41 us  [local_pass(): pl.pallas_call(functools.partial(pass_kernel, tile, exact), out_shape=(sh...]
    pallas_call x3, Pallas kernels: 97.1 us -> 90 us  [exchange(): pl.pallas_call(functools.partial(exchange_kernel, sizes, sums is not None...]
    unnamed x18 -> x20, local copies, waits for them, and re-layouts: 8.07 us -> 6.67 us
where the time goes in v2:
time: 101 us; the launch traced here: 100 us
  Pallas kernels  92.4 us (91%)
  local copies, waits for them, and re-layouts  6.67 us (7%)
  between operations  1.39 us (1%)
    pallas_call x3, Pallas kernels, exchange(): pl.pallas_call(functools.partial(exchange_kernel, sizes, sums is not None...  90 us
    unnamed x20, local copies, waits for them, and re-layouts  6.67 us
    pallas_call x2, Pallas kernels, local_pass(): pl.pallas_call(functools.partial(pass_kernel, tile, exact), out_shape=(sh...  2.41 us

profile of v2, /device:TPU:0, one launch (start us, length us, event | category | flops | bytes accessed | tf_op | source)
XLA Modules:
  0.0 100.4 jit_solution(6846270986105989478)
XLA Ops:
  1.3 0.0 copy-start.6
  1.3 1.0 %copy-done.6 = f32[2,2,128,256]{3,2,1,0:T(8,128)S(1)} copy-done((f32[2,2,128,256]{3,2,1,0:T(8,128)S(1)}, f32[2,2,128,256]{3,2,1,0:T(8,128)}, u32[]{:S(2)}) %copy-start.6) | copy-done | bytes 524312
  2.3 0.0 copy-start.3
  2.3 10.7 %exchange_0.1 = (f32[4,256,256]{2,1,0:T(8,128)S(1)}, f32[2,256,128]{2,1,0:T(8,128)S(1)}, f32[2,256,128]{2,1,0:T(8,128)S(1)}) custom-call(f32[4,128,256]{2,1,0:T(8,128)S(1)} %bitcast.10), custom_call_target="tpu_custom_call" | custom-call | bytes 33554432 | tf_op jit(solution)/shard_map/exchange_0/pallas_call | solution.py:584
  13.0 0.0 copy-start
  13.0 1.4 %copy-done = bf16[4,3,256,256]{3,2,1,0:T(8,128)(2,1)S(1)} copy-done((bf16[4,3,256,256]{3,2,1,0:T(8,128)(2,1)S(1)}, bf16[4,3,256,256]{3,2,1,0:T(8,128)(2,1)}, u32[]{:S(2)}) %copy-start) | copy-done | bytes 1572888
  14.4 0.0 copy-start.2
  14.4 1.0 %copy-done.2 = f32[4,2,128,128]{3,2,1,0:T(8,128)S(1)} copy-done((f32[4,2,128,128]{3,2,1,0:T(8,128)S(1)}, f32[4,2,128,128]{3,2,1,0:T(8,128)}, u32[]{:S(2)}) %copy-start.2) | copy-done | bytes 524312
  15.4 0.0 copy-start.4
  15.4 0.9 copy-done.4
  16.4 0.0 copy-start.7
  16.4 0.7 copy-done.7
  17.0 1.2 %local_pass.2 = (f32[4,256,512]{2,1,0:T(8,128)S(1)}, f32[2,256,128]{2,1,0:T(8,128)S(1)}, f32[2,256,128]{2,1,0:T(8,128)S(1)}, f32[9,128,128]{2,1,0:T(8,128)S(1)}) custom-call(s32[2,2]{1,0:T(2,128)S(1)} %bitcast.13, s32[1,1]{1,0:T(1,128)S(6)} %copy.10.cnt_ref, f32[4,256,256]{2,1,0:T(8,128)S(1)} %get-tuple-element.19.center_ref.refs_0_, ...), custom_call_target="tpu_custom_call" | custom-call | tf_op jit(solution)/shard_map/local_pass/pallas_call | solution.py:177
  18.2 0.0 copy-done.3
  18.2 0.0 copy-start.1
  18.3 0.0 copy-start.5
  18.3 0.0 copy-start.8
  18.3 46.8 %exchange_1.1 = (f32[4,256,256]{2,1,0:T(8,128)S(1)}, f32[2,256,128]{2,1,0:T(8,128)S(1)}, f32[2,256,128]{2,1,0:T(8,128)S(1)}, f32[8,128,128]{2,1,0:T(8,128)S(1)}) custom-call(f32[4,256,256]{2,1,0:T(8,128)S(1)} %get-tuple-element.19.center_ref.refs_0_, f32[4,256,512]{2,1,0:T(8,128)S(1)} %get-tuple-element.22.refs_1_, ...), custom_call_target="tpu_custom_call" | custom-call | bytes 33554432 | tf_op jit(solution)/shard_map/exchange_1/pallas_call | solution.py:584
  65.1 0.0 copy-done.1
  65.1 0.0 copy-done.5
  65.1 0.0 copy-done.8
  65.1 1.2 %local_pass.3 = (f32[4,256,512]{2,1,0:T(8,128)S(1)}, f32[2,256,128]{2,1,0:T(8,128)S(1)}, f32[2,256,128]{2,1,0:T(8,128)S(1)}, f32[9,128,128]{2,1,0:T(8,128)S(1)}) custom-call(s32[2,2]{1,0:T(2,128)S(1)} %bitcast.14, s32[1,1]{1,0:T(1,128)S(6)} %copy.10.cnt_ref, f32[4,256,256]{2,1,0:T(8,128)S(1)} %get-tuple-element.26.center_ref.refs_0_, ...), custom_call_target="tpu_custom_call" | custom-call | tf_op jit(solution)/shard_map/local_pass/pallas_call | solution.py:177
  66.3 32.5 %exchange_2.1 = (f32[4,128,256]{2,1,0:T(8,128)S(1)}, f32[8,128,128]{2,1,0:T(8,128)S(1)}) custom-call(f32[4,256,256]{2,1,0:T(8,128)S(1)} %get-tuple-element.26.center_ref.refs_0_, f32[4,256,512]{2,1,0:T(8,128)S(1)} %get-tuple-element.30.refs_1_, f32[2,256,128]{2,1,0:T(8,128)S(1)} %get-tuple-element.31.refs_2_, f32[2,256,128]{2,1,0:T(8,128)S(1)} %get-tuple-element.32.refs_3_, ...), custom_call_target="tpu_custom_call" | custom-call | bytes 33554432 | tf_op jit(solution)/shard_map/exchange_2/pallas_call | solution.py:584
  98.8 0.8 copy.11
  99.6 0.8 copy.12
Async XLA Ops:
  1.3 1.0 %copy-start.6 = (f32[2,2,128,256]{3,2,1,0:T(8,128)S(1)}, f32[2,2,128,256]{3,2,1,0:T(8,128)}, u32[]{:S(2)}) copy-start(f32[2,2,128,256]{3,2,1,0:T(8,128)} %param.6) | copy-start | bytes 1572868
  2.3 15.9 %copy-start.3 = (f32[4,2,128,128]{3,2,1,0:T(8,128)S(1)}, f32[4,2,128,128]{3,2,1,0:T(8,128)}, u32[]{:S(2)}) copy-start(f32[4,2,128,128]{3,2,1,0:T(8,128)} %param.7) | copy-start | bytes 1572868
  13.0 1.4 %copy-start = (bf16[4,3,256,256]{3,2,1,0:T(8,128)(2,1)S(1)}, bf16[4,3,256,256]{3,2,1,0:T(8,128)(2,1)}, u32[]{:S(2)}) copy-start(bf16[4,3,256,256]{3,2,1,0:T(8,128)(2,1)} %constant.2.clone.tab_ref) | copy-start | bytes 4718596
  14.4 1.0 %copy-start.2 = (f32[4,2,128,128]{3,2,1,0:T(8,128)S(1)}, f32[4,2,128,128]{3,2,1,0:T(8,128)}, u32[]{:S(2)}) copy-start(f32[4,2,128,128]{3,2,1,0:T(8,128)} %param.7) | copy-start | bytes 1572868
  15.4 0.9 copy-start.4
  16.4 0.7 copy-start.7
  18.2 46.8 %copy-start.1 = (bf16[4,3,256,256]{3,2,1,0:T(8,128)(2,1)S(1)}, bf16[4,3,256,256]{3,2,1,0:T(8,128)(2,1)}, u32[]{:S(2)}) copy-start(bf16[4,3,256,256]{3,2,1,0:T(8,128)(2,1)} %constant.2.clone.tab_ref) | copy-start | bytes 4718596
  18.3 46.8 %copy-start.5 = (f32[1,1,2,128,128]{4,3,2,1,0:T(8,128)S(1)}, f32[1,1,2,128,128]{4,3,2,1,0:T(8,128)}, u32[]{:S(2)}) copy-start(f32[1,1,2,128,128]{4,3,2,1,0:T(8,128)} %param.8) | copy-start | bytes 393220
  18.3 46.8 %copy-start.8 = (s32[1,1,2,2]{3,2,1,0:T(2,128)S(1)}, s32[1,1,2,2]{3,2,1,0:T(2,128)}, u32[]{:S(2)}) copy-start(s32[1,1,2,2]{3,2,1,0:T(2,128)} %param.9) | copy-start | bytes 52

commit v3 on v2

--- a/solution.py
+++ b/solution.py
@@ -11,6 +11,7 @@
 from jax.sharding import PartitionSpec as P
 
 ITERS = 2
+EIGHT = 8.0
 PASS_BYTES = 32 * 1024 * 1024
 EXCHANGE_BYTES = 24 * 1024 * 1024
 MESH = pl.DeviceIdType.MESH
@@ -24,12 +25,13 @@
 def transform_tables(width):
     index = np.arange(width)
     product = np.outer(index, index) % width
-    far = np.exp(-2j * math.pi * product / width) / math.sqrt(width)
+    turns = np.exp(-2j * math.pi * product / width)
+    far = turns / math.sqrt(width)
     frequency = (index + width // 2) % width - width // 2
     factor = np.exp(-4j * math.pi * frequency.astype(np.float64) ** 2 / width**2)
     step = far.conj() @ (factor[:, None] * far)
     step = (step + step.T) / 2
-    blocks = np.stack([real_block(far), real_block(far).T, real_block(step), real_block(step).T])
+    blocks = np.stack([real_block(turns / EIGHT), real_block(turns / EIGHT).T, real_block(step), real_block(step).T])
     parts = []
     for _ in range(3):
         parts.append(blocks.astype(ml_dtypes.bfloat16))
@@ -104,58 +106,89 @@
     lane = lax.broadcasted_iota(jnp.int32, (width, width), 1)
     tall_lane = lax.broadcasted_iota(jnp.int32, (width + 8, width), 1)
 
-    def slot(k, carry):
-        @pl.when(k < cnt_ref[0, 0])
-        def _():
+    factor = EIGHT * EIGHT / width
+    probe = lambda: [(modes_ref[2 * m], modes_ref[2 * m + 1]) for m in range(modes)]
+
+    class Slot:
+        def __init__(self, k):
+            self.k = k
             row = pos_ref[k, 0] - row0
             col = pos_ref[k, 1] - col0
-            base = pl.multiple_of((col // width) * width, width)
-            shift = col % width
-            top = pl.multiple_of((row // 8) * 8, 8)
-            down = row % 8
-            up = (width + 8 - down) % (width + 8)
-            back_shift = (width - shift) % width
-
-            def cut(p):
-                window = ext[p, pl.ds(top, width + 8), pl.ds(base, 2 * width)]
-                window = pltpu.roll(window, up, 0)[:width]
-                first = pltpu.roll(window[:, :width], back_shift, 1)
-                second = pltpu.roll(window[:, width:], back_shift, 1)
-                return jnp.where(lane < width - shift, first, second)
-
-            o0 = (cut(0), cut(1))
-            o1 = (cut(2), cut(3))
-            probe = [(modes_ref[2 * m], modes_ref[2 * m + 1]) for m in range(modes)]
-            waves = apply_transform(tab_ref, 2, [times(p, o0) for p in probe], exact)
-            far = apply_transform(tab_ref, 0, [times(w, o1) for w in waves], exact)
-            intensity = sum(r * r + i * i for r, i in far)
-            weight = 2.0 * (intensity - meas_ref[k])
-            grads = apply_transform(tab_ref, 1, [(weight * r, weight * i) for r, i in far], exact)
-
-            def add_patch(p, value):
-                value = jnp.concatenate([value, jnp.zeros((8, width), jnp.float32)], axis=0)
-                rolled = pltpu.roll(pltpu.roll(value, down, 0), shift, 1)
-                rows = pl.ds(top, width + 8)
-                grad_ref[p, rows, pl.ds(base, width)] += jnp.where(tall_lane >= shift, rolled, 0.0)
-                after = pl.multiple_of(base + width, width)
-                grad_ref[p, rows, pl.ds(after, width)] += jnp.where(tall_lane < shift, rolled, 0.0)
-
-            terms = [conj_times(w, g) for w, g in zip(waves, grads)]
-            add_patch(2, sum(t[0] for t in terms))
-            add_patch(3, sum(t[1] for t in terms))
-            grads = apply_transform(tab_ref, 3, [conj_times(o1, g) for g in grads], exact)
-            terms = [conj_times(p, g) for p, g in zip(probe, grads)]
-            add_patch(0, sum(t[0] for t in terms))
-            add_patch(1, sum(t[1] for t in terms))
+            self.base = pl.multiple_of((col // width) * width, width)
+            self.shift = col % width
+            self.top = pl.multiple_of((row // 8) * 8, 8)
+            self.down = row % 8
+            self.o0 = (self.cut(0), self.cut(1))
+            self.o1 = (self.cut(2), self.cut(3))
+
+        def cut(self, p):
+            window = ext[p, pl.ds(self.top, width + 8), pl.ds(self.base, 2 * width)]
+            window = pltpu.roll(window, (width + 8 - self.down) % (width + 8), 0)[:width]
+            back = (width - self.shift) % width
+            first = pltpu.roll(window[:, :width], back, 1)
+            second = pltpu.roll(window[:, width:], back, 1)
+            return jnp.where(lane < width - self.shift, first, second)
+
+        def add_patch(self, p, value):
+            value = jnp.concatenate([value, jnp.zeros((8, width), jnp.float32)], axis=0)
+            rolled = pltpu.roll(pltpu.roll(value, self.down, 0), self.shift, 1)
+            rows = pl.ds(self.top, width + 8)
+            grad_ref[p, rows, pl.ds(self.base, width)] += jnp.where(tall_lane >= self.shift, rolled, 0.0)
+            after = pl.multiple_of(self.base + width, width)
+            grad_ref[p, rows, pl.ds(after, width)] += jnp.where(tall_lane < self.shift, rolled, 0.0)
+
+        def forward(self):
+            self.waves = apply_transform(tab_ref, 2, [times(p, self.o0) for p in probe()], exact)
+
+        def far_field(self):
+            self.far = apply_transform(tab_ref, 0, [times(w, self.o1) for w in self.waves], False)
+
+        def far_back(self):
+            intensity = sum(r * r + i * i for r, i in self.far) * (factor * factor)
+            weight = (2.0 * factor * factor) * (intensity - meas_ref[self.k])
+            fields = [(weight * r, weight * i) for r, i in self.far]
+            self.grads = apply_transform(tab_ref, 1, fields, False)
+
+        def back(self):
+            terms = [conj_times(w, g) for w, g in zip(self.waves, self.grads)]
+            self.add_patch(2, sum(t[0] for t in terms))
+            self.add_patch(3, sum(t[1] for t in terms))
+            fields = [conj_times(self.o1, g) for g in self.grads]
+            self.grads = apply_transform(tab_ref, 3, fields, False)
+
+        def finish(self):
+            terms = [conj_times(p, g) for p, g in zip(probe(), self.grads)]
+            self.add_patch(0, sum(t[0] for t in terms))
+            self.add_patch(1, sum(t[1] for t in terms))
             for m in range(modes):
-                back = conj_times(o0, grads[m])
-                sums_ref[2 * m] += back[0]
-                sums_ref[2 * m + 1] += back[1]
-            sums_ref[2 * modes] += o0[0] * o0[0] + o0[1] * o0[1]
-
-        return carry
-
-    lax.fori_loop(0, slots, slot, 0)
+                term = conj_times(self.o0, self.grads[m])
+                sums_ref[2 * m] += term[0]
+                sums_ref[2 * m + 1] += term[1]
+            sums_ref[2 * modes] += self.o0[0] * self.o0[0] + self.o0[1] * self.o0[1]
+
+    def run(indices):
+        group = [Slot(k) for k in indices]
+        for phase in (Slot.forward, Slot.far_field, Slot.far_back, Slot.back, Slot.finish):
+            for one in group:
+                phase(one)
+
+    count = cnt_ref[0, 0]
+
+    @pl.when(count == slots)
+    def _():
+        run(range(slots))
+
+    @pl.when(count < slots)
+    def _():
+        def alone(k, carry):
+            @pl.when(k < count)
+            def _():
+                run([k])
+
+            return carry
+
+        lax.fori_loop(0, slots - 1, alone, 0)
+
     lane = lax.broadcasted_iota(jnp.int32, (grad_ref.shape[1], width), 1)
     for q in range(2):
         gl_ref[q] = jnp.where(
@@ -447,16 +480,13 @@
             (gr_ref.at[:, bottom, :], from_ul),
         ], rim_send, rim_recv)
         count = len(stages[0])
-        if has_halo:
-            rims.start()
         for part in parts:
             part.start(0)
         for part in parts:
             part.finish(0)
             if count > 1:
                 part.start(1)
-        if not has_halo:
-            rims.start()
+        rims.start()
         total[...] = grad_ref[:, inner, cols]
 
         def add_rim(d):

time: 101 us -> 93.2 us (0.923)
  Pallas kernels: 92.4 us -> 84.9 us
    pallas_call x3, Pallas kernels: 90 us -> 74.1 us  [exchange(): pl.pallas_call(functools.partial(exchange_kernel, sizes, sums is not None...]
    pallas_call x2, Pallas kernels: 2.41 us -> 10.8 us  [local_pass(): pl.pallas_call(functools.partial(pass_kernel, tile, exact), out_shape=(sh...]
where the time goes in v3:
time: 93.2 us; the launch traced here: 92.9 us
  Pallas kernels  84.9 us (91%)
  local copies, waits for them, and re-layouts  6.67 us (7%)
  between operations  1.39 us (1%)
    pallas_call x3, Pallas kernels, exchange(): pl.pallas_call(functools.partial(exchange_kernel, sizes, sums is not None...  74.1 us
    pallas_call x2, Pallas kernels, local_pass(): pl.pallas_call(functools.partial(pass_kernel, tile, exact), out_shape=(sh...  10.8 us
    unnamed x20, local copies, waits for them, and re-layouts  6.67 us

profile of v3, /device:TPU:0, one launch (start us, length us, event | category | flops | bytes accessed | tf_op | source)
XLA Modules:
  0.0 92.9 jit_solution(10939709496743054998)
XLA Ops:
  1.3 0.0 copy-start.6
  1.3 1.0 %copy-done.6 = f32[2,2,128,256]{3,2,1,0:T(8,128)S(1)} copy-done((f32[2,2,128,256]{3,2,1,0:T(8,128)S(1)}, f32[2,2,128,256]{3,2,1,0:T(8,128)}, u32[]{:S(2)}) %copy-start.6) | copy-done | bytes 524312
  2.3 0.0 copy-start.3
  2.3 10.7 %exchange_0.1 = (f32[4,256,256]{2,1,0:T(8,128)S(1)}, f32[2,256,128]{2,1,0:T(8,128)S(1)}, f32[2,256,128]{2,1,0:T(8,128)S(1)}) custom-call(f32[4,128,256]{2,1,0:T(8,128)S(1)} %bitcast.10), custom_call_target="tpu_custom_call" | custom-call | bytes 33554432 | tf_op jit(solution)/shard_map/exchange_0/pallas_call | solution.py:614
  13.0 0.0 copy-start
  13.0 1.4 %copy-done = bf16[4,3,256,256]{3,2,1,0:T(8,128)(2,1)S(1)} copy-done((bf16[4,3,256,256]{3,2,1,0:T(8,128)(2,1)S(1)}, bf16[4,3,256,256]{3,2,1,0:T(8,128)(2,1)}, u32[]{:S(2)}) %copy-start) | copy-done | bytes 1572888
  14.4 0.0 copy-start.2
  14.4 1.0 %copy-done.2 = f32[4,2,128,128]{3,2,1,0:T(8,128)S(1)} copy-done((f32[4,2,128,128]{3,2,1,0:T(8,128)S(1)}, f32[4,2,128,128]{3,2,1,0:T(8,128)}, u32[]{:S(2)}) %copy-start.2) | copy-done | bytes 524312
  15.4 0.0 copy-start.4
  15.4 0.9 copy-done.4
  16.4 0.0 copy-start.7
  16.4 0.7 copy-done.7
  17.0 5.4 %local_pass.2 = (f32[4,256,512]{2,1,0:T(8,128)S(1)}, f32[2,256,128]{2,1,0:T(8,128)S(1)}, f32[2,256,128]{2,1,0:T(8,128)S(1)}, f32[9,128,128]{2,1,0:T(8,128)S(1)}) custom-call(s32[2,2]{1,0:T(2,128)S(1)} %bitcast.13, s32[1,1]{1,0:T(1,128)S(6)} %copy.10.cnt_ref, f32[4,256,256]{2,1,0:T(8,128)S(1)} %get-tuple-element.19.center_ref.refs_0_, ...), custom_call_target="tpu_custom_call" | custom-call | tf_op jit(solution)/shard_map/local_pass/pallas_call | solution.py:210
  22.4 0.0 copy-done.3
  22.4 0.0 copy-start.1
  22.5 0.0 copy-start.5
  22.5 0.0 copy-start.8
  22.5 36.2 %exchange_1.1 = (f32[4,256,256]{2,1,0:T(8,128)S(1)}, f32[2,256,128]{2,1,0:T(8,128)S(1)}, f32[2,256,128]{2,1,0:T(8,128)S(1)}, f32[8,128,128]{2,1,0:T(8,128)S(1)}) custom-call(f32[4,256,256]{2,1,0:T(8,128)S(1)} %get-tuple-element.19.center_ref.refs_0_, f32[4,256,512]{2,1,0:T(8,128)S(1)} %get-tuple-element.22.refs_1_, ...), custom_call_target="tpu_custom_call" | custom-call | bytes 33554432 | tf_op jit(solution)/shard_map/exchange_1/pallas_call | solution.py:614
  58.7 0.0 copy-done.1
  58.7 0.0 copy-done.5
  58.7 0.0 copy-done.8
  58.7 5.4 %local_pass.3 = (f32[4,256,512]{2,1,0:T(8,128)S(1)}, f32[2,256,128]{2,1,0:T(8,128)S(1)}, f32[2,256,128]{2,1,0:T(8,128)S(1)}, f32[9,128,128]{2,1,0:T(8,128)S(1)}) custom-call(s32[2,2]{1,0:T(2,128)S(1)} %bitcast.14, s32[1,1]{1,0:T(1,128)S(6)} %copy.10.cnt_ref, f32[4,256,256]{2,1,0:T(8,128)S(1)} %get-tuple-element.26.center_ref.refs_0_, ...), custom_call_target="tpu_custom_call" | custom-call | tf_op jit(solution)/shard_map/local_pass/pallas_call | solution.py:210
  64.1 27.2 %exchange_2.1 = (f32[4,128,256]{2,1,0:T(8,128)S(1)}, f32[8,128,128]{2,1,0:T(8,128)S(1)}) custom-call(f32[4,256,256]{2,1,0:T(8,128)S(1)} %get-tuple-element.26.center_ref.refs_0_, f32[4,256,512]{2,1,0:T(8,128)S(1)} %get-tuple-element.30.refs_1_, f32[2,256,128]{2,1,0:T(8,128)S(1)} %get-tuple-element.31.refs_2_, f32[2,256,128]{2,1,0:T(8,128)S(1)} %get-tuple-element.32.refs_3_, ...), custom_call_target="tpu_custom_call" | custom-call | bytes 33554432 | tf_op jit(solution)/shard_map/exchange_2/pallas_call | solution.py:614
  91.4 0.8 copy.11
  92.2 0.8 copy.12
Async XLA Ops:
  1.3 1.0 %copy-start.6 = (f32[2,2,128,256]{3,2,1,0:T(8,128)S(1)}, f32[2,2,128,256]{3,2,1,0:T(8,128)}, u32[]{:S(2)}) copy-start(f32[2,2,128,256]{3,2,1,0:T(8,128)} %param.6) | copy-start | bytes 1572868
  2.3 20.1 %copy-start.3 = (f32[4,2,128,128]{3,2,1,0:T(8,128)S(1)}, f32[4,2,128,128]{3,2,1,0:T(8,128)}, u32[]{:S(2)}) copy-start(f32[4,2,128,128]{3,2,1,0:T(8,128)} %param.7) | copy-start | bytes 1572868
  13.0 1.4 %copy-start = (bf16[4,3,256,256]{3,2,1,0:T(8,128)(2,1)S(1)}, bf16[4,3,256,256]{3,2,1,0:T(8,128)(2,1)}, u32[]{:S(2)}) copy-start(bf16[4,3,256,256]{3,2,1,0:T(8,128)(2,1)} %constant.2.clone.tab_ref) | copy-start | bytes 4718596
  14.4 1.0 %copy-start.2 = (f32[4,2,128,128]{3,2,1,0:T(8,128)S(1)}, f32[4,2,128,128]{3,2,1,0:T(8,128)}, u32[]{:S(2)}) copy-start(f32[4,2,128,128]{3,2,1,0:T(8,128)} %param.7) | copy-start | bytes 1572868
  15.4 0.9 copy-start.4
  16.4 0.7 copy-start.7
  22.4 36.3 %copy-start.1 = (bf16[4,3,256,256]{3,2,1,0:T(8,128)(2,1)S(1)}, bf16[4,3,256,256]{3,2,1,0:T(8,128)(2,1)}, u32[]{:S(2)}) copy-start(bf16[4,3,256,256]{3,2,1,0:T(8,128)(2,1)} %constant.2.clone.tab_ref) | copy-start | bytes 4718596
  22.5 36.3 %copy-start.5 = (f32[1,1,2,128,128]{4,3,2,1,0:T(8,128)S(1)}, f32[1,1,2,128,128]{4,3,2,1,0:T(8,128)}, u32[]{:S(2)}) copy-start(f32[1,1,2,128,128]{4,3,2,1,0:T(8,128)} %param.8) | copy-start | bytes 393220
  22.5 36.3 %copy-start.8 = (s32[1,1,2,2]{3,2,1,0:T(2,128)S(1)}, s32[1,1,2,2]{3,2,1,0:T(2,128)}, u32[]{:S(2)}) copy-start(s32[1,1,2,2]{3,2,1,0:T(2,128)} %param.9) | copy-start | bytes 52

commit v4 on v3

--- a/solution.py
+++ b/solution.py
@@ -36,7 +36,7 @@
     for _ in range(3):
         parts.append(blocks.astype(ml_dtypes.bfloat16))
         blocks = blocks - parts[-1].astype(np.float64)
-    return np.stack(parts, axis=1)
+    return np.concatenate([np.concatenate(parts[:2]), parts[2][2:3]])
 
 
 def split_parts(value):
@@ -53,7 +53,7 @@
     pairs = [(0, high), (0, low), (1, high)] + ([(2, high)] if exact else [])
     total = None
     for part, operand in pairs:
-        table = tab_ref[place, part]
+        table = tab_ref[4 * part + (place if part < 2 else 0)]
         term = dot(table, operand) if table_first else dot(operand, table)
         total = term if total is None else total + term
     return total
@@ -90,8 +90,8 @@
     tile_rows, tile_cols = tile
     width = meas_ref.shape[-1]
     half = width // 2
-    slots = meas_ref.shape[0]
-    modes = modes_ref.shape[0] // 2
+    modes = sums_ref.shape[0] // 2
+    slots = meas_ref.shape[0] - 2 * modes
     last = width + tile_cols
     ext[:, :, width:last] = center_ref[...]
     for q in range(2):
@@ -145,7 +145,7 @@
 
         def far_back(self):
             intensity = sum(r * r + i * i for r, i in self.far) * (factor * factor)
-            weight = (2.0 * factor * factor) * (intensity - meas_ref[self.k])
+            weight = (2.0 * factor * factor) * (intensity - meas_ref[2 * modes + self.k])
             fields = [(weight * r, weight * i) for r, i in self.far]
             self.grads = apply_transform(tab_ref, 1, fields, False)
 
@@ -199,10 +199,10 @@
         )
 
 
-def local_pass(extended, modes, measured, positions, counts, tables, tile, exact):
+def local_pass(extended, modes, planes, given, positions, counts, tables, tile, exact):
     center, left, right = extended
     rows = center.shape[1]
-    width = measured.shape[-1]
+    width = given.shape[-1]
     wide = center.shape[2] + 2 * width
     smem = pl.BlockSpec(memory_space=pltpu.SMEM)
     vmem = pl.BlockSpec(memory_space=pltpu.VMEM)
@@ -213,14 +213,14 @@
             shape(4, rows, wide),
             shape(2, rows, width),
             shape(2, rows, width),
-            shape(modes.shape[0] + 1, width, width),
+            shape(planes + 1, width, width),
         ),
         in_specs=[smem, smem] + [vmem] * 6,
         out_specs=(vmem,) * 4,
         scratch_shapes=[pltpu.VMEM((4, rows, wide), jnp.float32)],
         compiler_params=pltpu.CompilerParams(vmem_limit_bytes=PASS_BYTES),
         name="local_pass",
-    )(positions, counts, center, left, right, modes, measured, tables)
+    )(positions, counts, center, left, right, modes, given, tables)
 
 
 class Neighbours:
@@ -630,12 +630,14 @@
     tile = objects.shape[2:]
     tables = jnp.asarray(transform_tables(width))
     modes = probe_modes.reshape(-1, width, width)
-    measured = intensities[0, 0]
+    planes = modes.shape[0]
+    given = jnp.concatenate([modes, intensities[0, 0]])
     extended = exchange(sizes, tile, width, 0, objects.reshape((4,) + tile))
     for step in range(ITERS):
         final = step == ITERS - 1
         sums = local_pass(
-            extended, modes, measured, positions[0, 0], counts, tables, tile, exact=not final
+            extended, modes if step else given, planes, given, positions[0, 0], counts, tables, tile,
+            exact=not final,
         )
         result = exchange(
             sizes, tile, width, step + 1, extended[0], tuple(sums) + (modes,),

time: 93.2 us -> 90.5 us (0.971)
  local copies, waits for them, and re-layouts: 6.67 us -> 3.37 us
  other arithmetic: 0 us -> 1.16 us
    pallas_call x2, Pallas kernels: 10.8 us -> 2.56 us  [local_pass(): pl.pallas_call(functools.partial(pass_kernel, tile, exact), out_shape=(sh...]
    pallas_call x3, Pallas kernels: 74.1 us -> 82.2 us  [exchange(): pl.pallas_call(functools.partial(exchange_kernel, sizes, sums is not None...]
    unnamed x20 -> x12, local copies, waits for them, and re-layouts: 6.67 us -> 3.37 us
    concatenate x0 -> x1, other arithmetic: none -> 1.16 us  [body(): given = jnp.concatenate([modes, intensities[0, 0]])]
where the time goes in v4:
time: 90.5 us; the launch traced here: 90.8 us
  Pallas kernels  84.8 us (94%)
  local copies, waits for them, and re-layouts  3.37 us (4%)
  between operations  1.48 us (2%)
  other arithmetic  1.16 us (1%)
    pallas_call x3, Pallas kernels, exchange(): pl.pallas_call(functools.partial(exchange_kernel, sizes, sums is not None...  82.2 us
    unnamed x12, local copies, waits for them, and re-layouts  3.37 us
    pallas_call x2, Pallas kernels, local_pass(): pl.pallas_call(functools.partial(pass_kernel, tile, exact), out_shape=(sh...  2.56 us

profile of v4, /device:TPU:0, one launch (start us, length us, event | category | flops | bytes accessed | tf_op | source)
XLA Modules:
  0.0 90.8 jit_solution(2773790123645474274)
XLA Ops:
  0.6 0.0 copy-start
  1.4 1.2 %pad_maximum_fusion.modes_ref.meas_ref = f32[10,128,128]{2,1,0:T(8,128)S(1)} fusion(f32[2,128,128]{2,1,0:T(8,128)} %bitcast.13, f32[8,128,128]{2,1,0:T(8,128)} %bitcast.6), kind=kLoop, calls=%fused_computation | loop fusion | flops 163840 | bytes 1310720 | tf_op jit(solution)/shard_map/concatenate | solution.py:634
  2.6 0.0 copy-start.2
  2.6 1.0 %copy-done.2 = f32[2,2,128,256]{3,2,1,0:T(8,128)S(1)} copy-done((f32[2,2,128,256]{3,2,1,0:T(8,128)S(1)}, f32[2,2,128,256]{3,2,1,0:T(8,128)}, u32[]{:S(2)}) %copy-start.2) | copy-done | bytes 524312
  3.6 10.7 %exchange_0.1 = (f32[4,256,256]{2,1,0:T(8,128)S(1)}, f32[2,256,128]{2,1,0:T(8,128)S(1)}, f32[2,256,128]{2,1,0:T(8,128)S(1)}) custom-call(f32[4,128,256]{2,1,0:T(8,128)S(1)} %bitcast.8), custom_call_target="tpu_custom_call" | custom-call | bytes 33554432 | tf_op jit(solution)/shard_map/exchange_0/pallas_call | solution.py:614
  14.3 0.0 copy-start.1
  14.3 0.0 copy-done
  14.3 0.0 copy-start.3
  14.3 0.7 copy-done.3
  15.0 1.2 %local_pass.2 = (f32[4,256,512]{2,1,0:T(8,128)S(1)}, f32[2,256,128]{2,1,0:T(8,128)S(1)}, f32[2,256,128]{2,1,0:T(8,128)S(1)}, f32[9,128,128]{2,1,0:T(8,128)S(1)}) custom-call(s32[2,2]{1,0:T(2,128)S(1)} %bitcast.11, s32[1,1]{1,0:T(1,128)S(6)} %copy.10.cnt_ref, f32[4,256,256]{2,1,0:T(8,128)S(1)} %get-tuple-element.19.center_ref.refs_0_, ...), custom_call_target="tpu_custom_call" | custom-call | tf_op jit(solution)/shard_map/local_pass/pallas_call | solution.py:210
  16.2 0.0 copy-done.1
  16.2 0.0 copy-start.4
  16.2 41.0 %exchange_1.1 = (f32[4,256,256]{2,1,0:T(8,128)S(1)}, f32[2,256,128]{2,1,0:T(8,128)S(1)}, f32[2,256,128]{2,1,0:T(8,128)S(1)}, f32[8,128,128]{2,1,0:T(8,128)S(1)}) custom-call(f32[4,256,256]{2,1,0:T(8,128)S(1)} %get-tuple-element.19.center_ref.refs_0_, f32[4,256,512]{2,1,0:T(8,128)S(1)} %get-tuple-element.22.refs_1_, ...), custom_call_target="tpu_custom_call" | custom-call | bytes 33554432 | tf_op jit(solution)/shard_map/exchange_1/pallas_call | solution.py:614
  57.2 0.0 copy-done.4
  57.2 1.4 %local_pass.3 = (f32[4,256,512]{2,1,0:T(8,128)S(1)}, f32[2,256,128]{2,1,0:T(8,128)S(1)}, f32[2,256,128]{2,1,0:T(8,128)S(1)}, f32[9,128,128]{2,1,0:T(8,128)S(1)}) custom-call(s32[2,2]{1,0:T(2,128)S(1)} %bitcast.12, s32[1,1]{1,0:T(1,128)S(6)} %copy.10.cnt_ref, f32[4,256,256]{2,1,0:T(8,128)S(1)} %get-tuple-element.26.center_ref.refs_0_, ...), custom_call_target="tpu_custom_call" | custom-call | tf_op jit(solution)/shard_map/local_pass/pallas_call | solution.py:210
  58.6 30.6 %exchange_2.1 = (f32[4,128,256]{2,1,0:T(8,128)S(1)}, f32[8,128,128]{2,1,0:T(8,128)S(1)}) custom-call(f32[4,256,256]{2,1,0:T(8,128)S(1)} %get-tuple-element.26.center_ref.refs_0_, f32[4,256,512]{2,1,0:T(8,128)S(1)} %get-tuple-element.30.refs_1_, f32[2,256,128]{2,1,0:T(8,128)S(1)} %get-tuple-element.31.refs_2_, f32[2,256,128]{2,1,0:T(8,128)S(1)} %get-tuple-element.32.refs_3_, ...), custom_call_target="tpu_custom_call" | custom-call | bytes 33554432 | tf_op jit(solution)/shard_map/exchange_2/pallas_call | solution.py:614
  89.2 0.8 copy.11
  90.0 0.8 copy.12
Async XLA Ops:
  0.6 13.7 %copy-start = (bf16[9,256,256]{2,1,0:T(8,128)(2,1)S(1)}, bf16[9,256,256]{2,1,0:T(8,128)(2,1)}, u32[]{:S(2)}) copy-start(bf16[9,256,256]{2,1,0:T(8,128)(2,1)} %constant.2.clone.tab_ref) | copy-start | bytes 3538948
  2.6 1.0 %copy-start.2 = (f32[2,2,128,256]{3,2,1,0:T(8,128)S(1)}, f32[2,2,128,256]{3,2,1,0:T(8,128)}, u32[]{:S(2)}) copy-start(f32[2,2,128,256]{3,2,1,0:T(8,128)} %param.6) | copy-start | bytes 1572868
  14.3 2.0 %copy-start.1 = (f32[4,2,128,128]{3,2,1,0:T(8,128)S(1)}, f32[4,2,128,128]{3,2,1,0:T(8,128)}, u32[]{:S(2)}) copy-start(f32[4,2,128,128]{3,2,1,0:T(8,128)} %param.7) | copy-start | bytes 1572868
  14.3 0.7 copy-start.3
  16.2 41.0 %copy-start.4 = (s32[1,1,2,2]{3,2,1,0:T(2,128)S(1)}, s32[1,1,2,2]{3,2,1,0:T(2,128)}, u32[]{:S(2)}) copy-start(s32[1,1,2,2]{3,2,1,0:T(2,128)} %param.9) | copy-start | bytes 52
